TPU v7x, 128 devices: a whole 4x4x4 slice. The times are simulated.
128 devices in a mesh: frame: 8 (over z, y_lo), space: 16 (over x, y_hi, core).
Axes of the slice: x: 4, y: 4 (y_hi: 2, y_lo: 2; y = y_hi * 2 + y_lo), z: 4, core: 2. Of those that a mesh axis runs over, the one named last changes fastest.
Arguments:
- hidden_in: bfloat16 [8, 4096, 1152], P('frame', 'space'), may hold values from -6 to 6
- query_space: bfloat16 [8, 4096, 1152], P('frame', 'space'), may hold values from -6 to 6
- key_space: bfloat16 [8, 4096, 1152], P('frame', 'space'), may hold values from -6 to 6
- value_space: bfloat16 [8, 4096, 1152], P('frame', 'space'), may hold values from -6 to 6
- cotangent: bfloat16 [8, 4096, 1152], P('frame', 'space'), may hold values from -6 to 6
- w_space_out: bfloat16 [1152, 1152], replicated, may hold values from -0.1875 to 0.1875
- w_time_qkv: bfloat16 [1152, 3456], replicated, may hold values from -1 to 1
- w_time_out: bfloat16 [1152, 1152], replicated, may hold values from -0.1875 to 0.1875
Outputs:
- block_out: bfloat16 [8, 4096, 1152], P('frame', 'space')
- grad_hidden: bfloat16 [8, 4096, 1152], P('frame', 'space')
- grad_query: bfloat16 [8, 4096, 1152], P('frame', 'space')
- grad_key: bfloat16 [8, 4096, 1152], P('frame', 'space')
- grad_value: bfloat16 [8, 4096, 1152], P('frame', 'space')
- grad_space_out: float32 [1152, 1152], P(('frame', 'space'))
- grad_time_qkv: float32 [1152, 3456], P(('frame', 'space'))
- grad_time_out: float32 [1152, 1152], P(('frame', 'space'))
All inputs are finite; a program needn't handle non-finite values.
Results may differ from a plain program's by a relative error of at most 0.02.
Values may be sent and summed in bfloat16 or wider, within the bound.
A program may use at most 256 MiB of HBM per device.

v0:
```python
import jax
import jax.numpy as jnp
from jax import lax
from jax.sharding import PartitionSpec as P

HEADS = 16
HD = 72


def attend_forward(query, key_rows, value_rows):
    seq_length, head_count, head_dim = query.shape
    score_scale = head_dim ** (-0.5)
    block_rows = min(512, seq_length)
    block_count = seq_length // block_rows
    query_blocks = query.reshape(block_count, block_rows, head_count, head_dim)

    def one_block(query_block):
        scores = (
            jnp.einsum("qhe,khe->hqk", query_block, key_rows, preferred_element_type=jnp.float32)
            * score_scale
        )
        row_max = jnp.max(scores, axis=-1, keepdims=True)
        exp_rows = jnp.exp(scores - row_max)
        row_sum = jnp.sum(exp_rows, axis=-1, keepdims=True)
        prob_bf = (exp_rows / row_sum).astype(jnp.bfloat16)
        mixed_out = jnp.einsum(
            "hqk,khe->qhe", prob_bf, value_rows, preferred_element_type=jnp.float32
        )
        return (mixed_out.astype(jnp.bfloat16), (row_max + jnp.log(row_sum))[..., 0])

    mixed_out, logsum = lax.map(one_block, query_blocks)
    return (mixed_out.reshape(seq_length, head_count, head_dim), logsum)


def attend_backward(query, key_rows, value_rows, logsum, grad_mixed):
    seq_length, head_count, head_dim = query.shape
    score_scale = head_dim ** (-0.5)
    block_rows = min(512, seq_length)
    block_count = seq_length // block_rows
    query_blocks = query.reshape(block_count, block_rows, head_count, head_dim)
    grad_blocks = grad_mixed.reshape(block_count, block_rows, head_count, head_dim)

    def backward_step(state, inputs):
        acc_key, acc_value = state
        query_block, grad_block, logsum_block = inputs
        scores = (
            jnp.einsum("qhe,khe->hqk", query_block, key_rows, preferred_element_type=jnp.float32)
            * score_scale
        )
        probs = jnp.exp(scores - logsum_block[..., None])
        grad_probs = jnp.einsum(
            "qhe,khe->hqk", grad_block, value_rows, preferred_element_type=jnp.float32
        )
        row_inner = jnp.sum(probs * grad_probs, axis=-1, keepdims=True)
        grad_scores = (probs * (grad_probs - row_inner) * score_scale).astype(jnp.bfloat16)
        grad_query = jnp.einsum(
            "hqk,khe->qhe", grad_scores, key_rows, preferred_element_type=jnp.float32
        ).astype(jnp.bfloat16)
        acc_key = acc_key + jnp.einsum(
            "hqk,qhe->khe", grad_scores, query_block, preferred_element_type=jnp.float32
        )
        acc_value = acc_value + jnp.einsum(
            "hqk,qhe->khe",
            probs.astype(jnp.bfloat16),
            grad_block,
            preferred_element_type=jnp.float32,
        )
        return ((acc_key, acc_value), grad_query)

    zero_acc = jnp.zeros((seq_length, head_count, head_dim), jnp.float32)
    (acc_key, acc_value), grad_query = lax.scan(
        backward_step, (zero_acc, zero_acc), (query_blocks, grad_blocks, logsum)
    )
    return (
        grad_query.reshape(seq_length, head_count, head_dim),
        acc_key.astype(jnp.bfloat16),
        acc_value.astype(jnp.bfloat16),
    )


def to_heads(stacked):
    return lax.all_to_all(stacked, "space", split_axis=3, concat_axis=2, tiled=True)


def from_heads(stacked):
    return lax.all_to_all(stacked, "space", split_axis=2, concat_axis=3, tiled=True)


def to_columns(stacked):
    return lax.all_to_all(stacked, "frame", split_axis=2, concat_axis=1, tiled=True)


def from_columns(stacked):
    return lax.all_to_all(stacked, "frame", split_axis=1, concat_axis=2, tiled=True)


def project_three(rows, w_time_split):
    model_width = rows.shape[-1]
    flat_rows = rows.reshape(-1, model_width)
    projected = jnp.einsum(
        "td,dcw->ctw", flat_rows, w_time_split, preferred_element_type=jnp.float32
    )
    return projected.astype(jnp.bfloat16).reshape((3,) + rows.shape)


def time_forward(projected):
    frames_all, columns, model_width = projected.shape[1:]
    split_rows = projected.reshape(3, frames_all, columns, HEADS, HD)
    mixed_time, logsum_time = jax.vmap(attend_forward, in_axes=1, out_axes=(1, 0))(
        split_rows[0], split_rows[1], split_rows[2]
    )
    return (mixed_time.reshape(frames_all, columns, model_width), logsum_time)


def time_backward(projected, logsum_time, grad_mixed):
    frames_all, columns, model_width = projected.shape[1:]
    split_rows = projected.reshape(3, frames_all, columns, HEADS, HD)
    grad_split = grad_mixed.reshape(frames_all, columns, HEADS, HD)
    grads = jax.vmap(attend_backward, in_axes=(1, 1, 1, 0, 1), out_axes=1)(
        split_rows[0], split_rows[1], split_rows[2], logsum_time, grad_split
    )
    return jnp.stack(grads).reshape(3, frames_all, columns, model_width)


def temporal_grads(hidden_rows, cot_rows, attn_rows, grad_proj, w_time_split):
    model_width = hidden_rows.shape[-1]
    grad_time_out = jnp.einsum(
        "td,tw->dw",
        attn_rows.reshape(-1, model_width),
        cot_rows.reshape(-1, model_width),
        preferred_element_type=jnp.float32,
    )
    proj_flat = grad_proj.reshape(3, -1, model_width)
    grad_time_qkv = jnp.einsum(
        "td,ctw->dcw",
        hidden_rows.reshape(-1, model_width),
        proj_flat,
        preferred_element_type=jnp.float32,
    ).reshape(model_width, 3 * model_width)
    grad_rows = cot_rows.reshape(-1, model_width).astype(jnp.float32) + jnp.einsum(
        "ctw,dcw->td", proj_flat, w_time_split, preferred_element_type=jnp.float32
    )
    return (grad_time_out, grad_time_qkv, grad_rows.astype(jnp.bfloat16).reshape(hidden_rows.shape))


def add_projection(base_rows, attn_rows, weight):
    model_width = base_rows.shape[-1]
    product = jnp.dot(
        attn_rows.reshape(-1, model_width), weight, preferred_element_type=jnp.float32
    )
    return (base_rows.astype(jnp.float32) + product.reshape(base_rows.shape)).astype(jnp.bfloat16)


def grad_through(grad_rows, weight):
    model_width = grad_rows.shape[-1]
    product = jnp.dot(
        grad_rows.reshape(-1, model_width), weight.T, preferred_element_type=jnp.float32
    )
    return product.astype(jnp.bfloat16).reshape(grad_rows.shape)


def shards(
    hidden_in, query_space, key_space, value_space, cotangent, w_space_out, w_time_qkv, w_time_out
):
    frames_dev, tile_rows, model_width = hidden_in.shape
    heads_dev = HEADS // lax.axis_size("space")
    w_time_split = w_time_qkv.reshape(model_width, 3, model_width)
    head_rows = to_heads(jnp.stack([query_space, key_space, value_space]))
    seq_length = head_rows.shape[2]
    head_split = head_rows.reshape(3, frames_dev, seq_length, heads_dev, HD)
    mixed_heads, logsum_space = jax.vmap(attend_forward)(
        head_split[0], head_split[1], head_split[2]
    )
    attn_space = from_heads(mixed_heads.reshape(1, frames_dev, seq_length, heads_dev * HD))[0]
    hidden = add_projection(hidden_in, attn_space, w_space_out)
    projected = to_columns(project_three(hidden, w_time_split))
    attn_cols, logsum_time = time_forward(projected)
    attn_time = from_columns(attn_cols[None])[0]
    block_out = add_projection(hidden, attn_time, w_time_out)
    grad_attn_time = grad_through(cotangent, w_time_out)
    grad_attn_cols = to_columns(grad_attn_time[None])[0]
    grad_proj_cols = time_backward(projected, logsum_time, grad_attn_cols)
    grad_proj = from_columns(grad_proj_cols)
    grad_time_out, grad_time_qkv, grad_hidden = temporal_grads(
        hidden, cotangent, attn_time, grad_proj, w_time_split
    )
    grad_space_out = jnp.einsum(
        "td,tw->dw",
        attn_space.reshape(-1, model_width),
        grad_hidden.reshape(-1, model_width),
        preferred_element_type=jnp.float32,
    )
    grad_attn_space = grad_through(grad_hidden, w_space_out)
    grad_heads = to_heads(grad_attn_space[None])[0].reshape(frames_dev, seq_length, heads_dev, HD)
    space_grads = jax.vmap(attend_backward)(
        head_split[0], head_split[1], head_split[2], logsum_space, grad_heads
    )
    returned_space = from_heads(
        jnp.stack(space_grads).reshape(3, frames_dev, seq_length, heads_dev * HD)
    )
    sum_space_out, sum_time_qkv, sum_time_out = (
        lax.psum_scatter(grad_space_out, ("frame", "space"), scatter_dimension=0, tiled=True),
        lax.psum_scatter(grad_time_qkv, ("frame", "space"), scatter_dimension=0, tiled=True),
        lax.psum_scatter(grad_time_out, ("frame", "space"), scatter_dimension=0, tiled=True),
    )
    return (
        block_out,
        grad_hidden,
        returned_space[0],
        returned_space[1],
        returned_space[2],
        sum_space_out,
        sum_time_qkv,
        sum_time_out,
    )


def solution(mesh):
    placed = (
        P("frame", "space", None),
        P("frame", "space", None),
        P("frame", "space", None),
        P("frame", "space", None),
        P("frame", "space", None),
        P(),
        P(),
        P(),
    )
    return jax.shard_map(
        shards,
        mesh=mesh,
        in_specs=placed,
        out_specs=(
            P("frame", "space", None),
            P("frame", "space", None),
            P("frame", "space", None),
            P("frame", "space", None),
            P("frame", "space", None),
            P(("frame", "space"), None),
            P(("frame", "space"), None),
            P(("frame", "space"), None),
        ),
        check_vma=False,
    )
```

profile of v0, /device:TPU:1, one launch (start us, length us, event | category | flops | bytes accessed | tf_op | source)
XLA Modules:
  0.0 729.5 jit_solution(10068346163972982407)
XLA Ops:
  15.1 8.4 %all-to-all-start = ((bf16[3,1,256,1152]{2,0,1,3:T(4,128)(2,1)}), bf16[3,1,256,1152]{2,0,1,3:T(4,128)(2,1)}, u32[]{:S(2)}, u32[]{:S(2)}) async-start(bf16[3,1,256,1152]{2,0,1,3:T(4,128)(2,1)} %copy.93), calls=%async_computation | async-start | bytes 4718592 | tf_op jit(solution)/shard_map/all_to_all | solution.py:82
  23.5 31.4 %all-to-all-done = bf16[3,1,256,1152]{2,0,1,3:T(4,128)(2,1)} async-done(((bf16[3,1,256,1152]{2,0,1,3:T(4,128)(2,1)}), bf16[3,1,256,1152]{2,0,1,3:T(4,128)(2,1)}, u32[]{:S(2)}, u32[]{:S(2)}) %all-to-all-start) | async-done | bytes 1769504 | tf_op jit(solution)/shard_map/all_to_all | solution.py:82
  70.0 53.8 %while.5 = (s32[]{:T(128)}, bf16[8,1,512,1,72]{2,4,3,1,0:T(8,128)(2,1)}, f32[8,1,1,512]{3,2,1,0:T(1,128)S(1)}, bf16[8,1,512,1,72]{2,4,3,1,0:T(8,128)(2,1)}, bf16...) while((s32[]{:T(128)}, bf16[8,1,512,1,72]{2,4,3,1,0:T(8,128)(2,1)}, ...), condition=%wide.region_3.4_spmd, body=%wide.region_0.3_spmd.sunk | while | flops 622890496 | bytes 28872828 | solution.py:31
  125.9 6.9 reshape.241
  133.3 24.4 %reduce.14 = bf16[4096,72]{1,0:T(8,128)(2,1)} reduce(bf16[4096,1,1,72]{3,2,1,0:T(2,128)(2,1)} %bitcast.274, bf16[]{:T(256)} %broadcast.86), dimensions={1,2}, to_apply=%bitcast.197.reduce_sub_computation | reduce | bytes 1179650
  162.4 6.4 all-to-all-start.1
  168.8 11.5 %copy.103 = bf16[1152,3456]{0,1:T(8,128)(2,1)} copy(bf16[1152,3456]{1,0:T(8,128)(2,1)} %param.18) | data formatting | bytes 15925248 | tf_op args[6]
  198.9 7.1 reshape.247
  213.8 6.0 fusion.34
  240.9 16.1 %all-to-all-done.2 = bf16[3,1,256,1152]{3,0,1,2:T(4,128)(2,1)} async-done(((bf16[3,1,256,1152]{3,0,1,2:T(4,128)(2,1)}), bf16[3,1,256,1152]{3,0,1,2:T(4,128)(2,1)}, u32[]{:S(2)}, u32[]{:S(2)}) %all-to-all-start.2) | async-done | bytes 1769504 | tf_op jit(solution)/shard_map/all_to_all | solution.py:90
  257.0 13.9 %slice_reduce_fusion.2 = (bf16[256,1152]{1,0:T(8,128)(2,1)}, bf16[256,1152]{1,0:T(8,128)(2,1)}, bf16[256,1152]{1,0:T(8,128)(2,1)}) fusion(bf16[3,1,256,1152]{3,0,1,2:T(4,128)(2,1)} %all-to-all-done.2), kind=kLoop, calls=%fused_computation.83 | loop fusion | bytes 3538944 | tf_op jit(solution)/shard_map/slice | solution.py:110
  306.9 6.6 fusion.49
  318.7 6.6 fusion.48
  343.6 16.2 %all-to-all-done.5 = bf16[3,8,32,1152]{3,2,0,1:T(8,128)(2,1)} async-done(((bf16[3,8,32,1152]{3,2,0,1:T(8,128)(2,1)}), bf16[3,8,32,1152]{3,2,0,1:T(8,128)(2,1)}, u32[]{:S(2)}, u32[]{:S(2)}) %all-to-all-start.5) | async-done | bytes 1769504 | tf_op jit(solution)/shard_map/all_to_all | solution.py:94
  361.5 6.5 fusion.38
  375.3 6.3 reduce.16
  382.5 11.0 %all-to-all-start.6 = ((bf16[16,2,9216]{2,1,0:T(2,128)(2,1)}), bf16[16,2,9216]{2,1,0:T(2,128)(2,1)}, u32[]{:S(2)}, u32[]{:S(2)}) async-start(bf16[16,2,9216]{2,1,0:T(2,128)(2,1)} %reshape.250), calls=%async_computation.6 | async-start | bytes 1179648 | tf_op jit(solution)/shard_map/all_to_all | solution.py:82
  396.4 7.9 %fusion.79 = f32[1152,3456]{1,0:T(8,128)} fusion(bf16[3456,256]{1,0:T(8,128)(2,1)S(1)} %bitcast.280, bf16[1,256,1152]{2,1,0:T(8,128)(2,1)S(1)} %copy-done.15), kind=kOutput, calls=%fused_computation.110 | convolution fusion | flops 2038431744 | bytes 18284544 | tf_op jit(solution)/shard_map/td,ctw->dcw/dot_general | solution.py:134
  413.5 237.0 %while.6 = (s32[]{:T(128)}, f32[1,4096,1,72]{1,3,2,0:T(8,128)S(1)}, f32[1,4096,1,72]{1,3,2,0:T(8,128)S(1)}, bf16[8,1,512,1,72]{2,4,3,1,0:T(8,128)(2,1)}, bf16[8,...) while((s32[]{:T(128)}, ...), condition=%wide.region_9.10_spmd.clone, body=%wide.region_7.9_spmd.clone.sunk | while | flops 1530039808 | bytes 120113376 | solution.py:71
  422.0 10.9 %multiply_convert_fusion.3 = bf16[512,4096]{1,0:T(8,128)(2,1)} fusion(f32[512,4096]{1,0:T(8,128)} %get-tuple-element.389, f32[512,4096]{1,0:T(8,128)} %copy-done.2, f32[512]{0:T(512)S(1)} %get-tuple-element.390), kind=kLoop, calls=%fused_computation.17.clone.1 | loop fusion | flops 8388608 | bytes 20973568 | tf_op jit(solution)/shard_map/vmap()/while/body/eval_jaxpr/convert_element_type | solution.py:55
  445.9 6.0 multiply_reduce_fusion.7
  453.0 10.8 %multiply_convert_fusion.3 = bf16[512,4096]{1,0:T(8,128)(2,1)} fusion(f32[512,4096]{1,0:T(8,128)} %get-tuple-element.389, f32[512,4096]{1,0:T(8,128)} %copy-done.2, f32[512]{0:T(512)S(1)} %get-tuple-element.390), kind=kLoop, calls=%fused_computation.17.clone.1 | loop fusion | flops 8388608 | bytes 20973568 | tf_op jit(solution)/shard_map/vmap()/while/body/eval_jaxpr/convert_element_type | solution.py:55
  482.7 10.8 %multiply_convert_fusion.3 = bf16[512,4096]{1,0:T(8,128)(2,1)} fusion(f32[512,4096]{1,0:T(8,128)} %get-tuple-element.389, f32[512,4096]{1,0:T(8,128)} %copy-done.2, f32[512]{0:T(512)S(1)} %get-tuple-element.390), kind=kLoop, calls=%fused_computation.17.clone.1 | loop fusion | flops 8388608 | bytes 20973568 | tf_op jit(solution)/shard_map/vmap()/while/body/eval_jaxpr/convert_element_type | solution.py:55
  511.8 10.2 %multiply_convert_fusion.3 = bf16[512,4096]{1,0:T(8,128)(2,1)} fusion(f32[512,4096]{1,0:T(8,128)} %get-tuple-element.389, f32[512,4096]{1,0:T(8,128)} %copy-done.2, f32[512]{0:T(512)S(1)} %get-tuple-element.390), kind=kLoop, calls=%fused_computation.17.clone.1 | loop fusion | flops 8388608 | bytes 20973568 | tf_op jit(solution)/shard_map/vmap()/while/body/eval_jaxpr/convert_element_type | solution.py:55
  540.2 10.2 %multiply_convert_fusion.3 = bf16[512,4096]{1,0:T(8,128)(2,1)} fusion(f32[512,4096]{1,0:T(8,128)} %get-tuple-element.389, f32[512,4096]{1,0:T(8,128)} %copy-done.2, f32[512]{0:T(512)S(1)} %get-tuple-element.390), kind=kLoop, calls=%fused_computation.17.clone.1 | loop fusion | flops 8388608 | bytes 20973568 | tf_op jit(solution)/shard_map/vmap()/while/body/eval_jaxpr/convert_element_type | solution.py:55
  569.0 10.2 %multiply_convert_fusion.3 = bf16[512,4096]{1,0:T(8,128)(2,1)} fusion(f32[512,4096]{1,0:T(8,128)} %get-tuple-element.389, f32[512,4096]{1,0:T(8,128)} %copy-done.2, f32[512]{0:T(512)S(1)} %get-tuple-element.390), kind=kLoop, calls=%fused_computation.17.clone.1 | loop fusion | flops 8388608 | bytes 20973568 | tf_op jit(solution)/shard_map/vmap()/while/body/eval_jaxpr/convert_element_type | solution.py:55
  598.8 11.1 %multiply_convert_fusion.3 = bf16[512,4096]{1,0:T(8,128)(2,1)} fusion(f32[512,4096]{1,0:T(8,128)} %get-tuple-element.389, f32[512,4096]{1,0:T(8,128)} %copy-done.2, f32[512]{0:T(512)S(1)} %get-tuple-element.390), kind=kLoop, calls=%fused_computation.17.clone.1 | loop fusion | flops 8388608 | bytes 20973568 | tf_op jit(solution)/shard_map/vmap()/while/body/eval_jaxpr/convert_element_type | solution.py:55
  629.7 10.9 %multiply_convert_fusion.3 = bf16[512,4096]{1,0:T(8,128)(2,1)} fusion(f32[512,4096]{1,0:T(8,128)} %get-tuple-element.389, f32[512,4096]{1,0:T(8,128)} %copy-done.2, f32[512]{0:T(512)S(1)} %get-tuple-element.390), kind=kLoop, calls=%fused_computation.17.clone.1 | loop fusion | flops 8388608 | bytes 20973568 | tf_op jit(solution)/shard_map/vmap()/while/body/eval_jaxpr/convert_element_type | solution.py:55
  658.9 9.0 %reshape.252 = bf16[16,2,27648]{2,1,0:T(2,128)(2,1)} reshape(bf16[4096,1,3,72]{3,2,1,0:T(4,128)(2,1)} %bitcast.272) | data formatting | bytes 3538944
  667.9 6.5 all-to-all-start.7
  678.1 21.2 %all-to-all-done.7 = bf16[16,2,27648]{2,1,0:T(2,128)(2,1)S(1)} async-done(((bf16[16,2,27648]{2,1,0:T(2,128)(2,1)}), bf16[16,2,27648]{2,1,0:T(2,128)(2,1)S(1)}, u32[]{:S(2)}, u32[]{:S(2)}) %all-to-all-start.7) | async-done | bytes 1769504 | tf_op jit(solution)/shard_map/all_to_all | solution.py:86
  699.3 7.5 %reshape.253 = bf16[4096,1,3,72]{3,2,1,0:T(4,128)(2,1)} reshape(bf16[16,2,27648]{2,1,0:T(2,128)(2,1)S(1)} %all-to-all-done.7) | data formatting | bytes 3538944
  (262 shorter events, 385.8 us)
Async XLA Ops:
  7.2 205.5 %copy-start = (bf16[1152,1152]{1,0:T(8,128)(2,1)S(1)}, bf16[1152,1152]{1,0:T(8,128)(2,1)}, u32[]{:S(2)}) copy-start(bf16[1152,1152]{1,0:T(8,128)(2,1)} %param.17) | copy-start | bytes 7962628
  15.1 39.8 %all-to-all-start = ((bf16[3,1,256,1152]{2,0,1,3:T(4,128)(2,1)}), bf16[3,1,256,1152]{2,0,1,3:T(4,128)(2,1)}, u32[]{:S(2)}, u32[]{:S(2)}) async-start(bf16[3,1,256,1152]{2,0,1,3:T(4,128)(2,1)} %copy.93), calls=%async_computation | async-start | bytes 4718592 | tf_op jit(solution)/shard_map/all_to_all | solution.py:82
  162.4 31.3 %all-to-all-start.1 = ((bf16[16,2,9216]{2,1,0:T(2,128)(2,1)}), bf16[16,2,9216]{2,1,0:T(2,128)(2,1)}, u32[]{:S(2)}, u32[]{:S(2)}) async-start(bf16[16,2,9216]{2,1,0:T(2,128)(2,1)} %reshape.246), calls=%async_computation.1 | async-start | bytes 1179648 | tf_op jit(solution)/shard_map/all_to_all | solution.py:86
  193.7 29.0 %all-to-all-start.4 = ((bf16[8,2,18432]{2,1,0:T(2,128)(2,1)}), bf16[8,2,18432]{2,1,0:T(2,128)(2,1)}, u32[]{:S(2)}, u32[]{:S(2)}) async-start(bf16[8,2,18432]{2,1,0:T(2,128)(2,1)} %reshape.248), calls=%async_computation.4 | async-start | bytes 1179648 | tf_op jit(solution)/shard_map/all_to_all | solution.py:90
  213.8 6.1 copy-start.14
  222.8 34.2 %all-to-all-start.2 = ((bf16[3,1,256,1152]{3,0,1,2:T(4,128)(2,1)}), bf16[3,1,256,1152]{3,0,1,2:T(4,128)(2,1)}, u32[]{:S(2)}, u32[]{:S(2)}) async-start(bf16[3,1,256,1152]{3,0,1,2:T(4,128)(2,1)} %copy.105), calls=%async_computation.2 | async-start | bytes 4718592 | tf_op jit(solution)/shard_map/all_to_all | solution.py:90
  292.7 41.0 %all-to-all-start.3 = ((bf16[1,8,32,1152]{3,2,0,1:T(8,128)(2,1)}), bf16[1,8,32,1152]{3,2,0,1:T(8,128)(2,1)}, u32[]{:S(2)}, u32[]{:S(2)}) async-start(bf16[1,8,32,1152]{3,2,0,1:T(8,128)(2,1)} %bitcast.288), calls=%async_computation.3 | async-start | bytes 1179648 | tf_op jit(solution)/shard_map/all_to_all | solution.py:94
  333.7 26.1 %all-to-all-start.5 = ((bf16[3,8,32,1152]{3,2,0,1:T(8,128)(2,1)}), bf16[3,8,32,1152]{3,2,0,1:T(8,128)(2,1)}, u32[]{:S(2)}, u32[]{:S(2)}) async-start(bf16[3,8,32,1152]{3,2,0,1:T(8,128)(2,1)} %copy.118), calls=%async_computation.5 | async-start | bytes 3538944 | tf_op jit(solution)/shard_map/all_to_all | solution.py:94
  361.5 6.5 copy-start.12
  382.5 13.9 %copy-start.15 = (bf16[1,256,1152]{2,1,0:T(8,128)(2,1)S(1)}, bf16[1,256,1152]{2,1,0:T(8,128)(2,1)}, u32[]{:S(2)}) copy-start(bf16[1,256,1152]{2,1,0:T(8,128)(2,1)} %copy-done.14) | copy-start | bytes 1769476
  382.5 22.8 %all-to-all-start.6 = ((bf16[16,2,9216]{2,1,0:T(2,128)(2,1)}), bf16[16,2,9216]{2,1,0:T(2,128)(2,1)}, u32[]{:S(2)}, u32[]{:S(2)}) async-start(bf16[16,2,9216]{2,1,0:T(2,128)(2,1)} %reshape.250), calls=%async_computation.6 | async-start | bytes 1179648 | tf_op jit(solution)/shard_map/all_to_all | solution.py:82
  393.5 325.4 %all-reduce.6.cloned.1.call-start = ((), (), s32[]{:S(2)}) async-start(), calls=%async_computation.8 | async-start | bytes 53084160
  407.6 5.9 copy-start.4
  407.6 5.9 copy-start.5
  415.9 6.0 copy-start.2
  436.4 5.1 copy-start.3
  445.9 7.1 copy-start.2
  467.2 5.2 copy-start.3
  476.9 5.8 copy-start.2
  496.8 4.8 copy-start.3
  506.0 5.8 copy-start.2
  525.3 4.6 copy-start.3
  534.3 5.8 copy-start.2
  553.6 5.2 copy-start.3
  563.2 5.8 copy-start.2
  583.1 5.1 copy-start.3
  592.7 6.1 copy-start.2
  613.7 5.2 copy-start.3
  623.4 6.3 copy-start.2
  667.9 6.5 copy-start.16
  667.9 31.4 %all-to-all-start.7 = ((bf16[16,2,27648]{2,1,0:T(2,128)(2,1)}), bf16[16,2,27648]{2,1,0:T(2,128)(2,1)S(1)}, u32[]{:S(2)}, u32[]{:S(2)}) async-start(bf16[16,2,27648]{2,1,0:T(2,128)(2,1)} %reshape.252), calls=%async_computation.7 | async-start | bytes 3538944 | tf_op jit(solution)/shard_map/all_to_all | solution.py:86
  713.5 8.7 %copy-start.1 = (bf16[1152,1152]{1,0:T(8,128)(2,1)S(1)}, bf16[1152,1152]{1,0:T(8,128)(2,1)}, u32[]{:S(2)}) copy-start(bf16[1152,1152]{1,0:T(8,128)(2,1)} %param.17) | copy-start | bytes 7962628
  (20 other events, 42.9 us)
Sparse Core Ops, SparseCore 0:
  404.5 234.1 all-reduce.5
where the time goes:
time: 743 us; the launch traced here: 730 us
  matrix products  251 us (34%)
  local copies, waits for them, and re-layouts  185 us (25%)
  other arithmetic  140 us (19%)
  waiting for transfers between devices  85.8 us (12%)
  starting transfers between devices  52.8 us (7%)
  between operations  14.9 us (2%)
    convert_element_type x8, other arithmetic, backward_step(): (probs * (grad_probs - row_inner) * score_scale).astype(jnp.bfloat16)  85.1 us
    unnamed x56, local copies, waits for them, and re-layouts  63.7 us
    dot_general x8, matrix products, backward_step(): jnp.einsum('qhe,khe->hqk', query_block, key_rows, preferred_element_type=...  46.8 us
    dot_general x9, matrix products, backward_step(): jnp.einsum('hqk,qhe->khe', probs.astype(jnp.bfloat16), grad_block, prefer...  39.7 us
    unnamed x5, other arithmetic  36.7 us
    dot_general x9, matrix products, backward_step(): jnp.einsum('hqk,qhe->khe', grad_scores, query_block, preferred_element_ty...  34.3 us
    all_to_all x2, waiting for transfers between devices, to_heads(): lax.all_to_all(stacked, 'space', split_axis=3, concat_axis=2, tiled=True)  32.3 us
    dot_general x9, matrix products, one_block(): jnp.einsum('hqk,khe->qhe', prob_bf, value_rows, preferred_element_type=jn...  24.7 us
  transfers between devices with their start and end apart: 9, of which 5 were waited for; matrix products, arithmetic and copies ran while one was open for 54% of the time, Pallas kernels for 0%

commit v1 on v0

v1 whole, which is shorter than its diff:
```python
import jax
import jax.numpy as jnp
from jax import lax
from jax.experimental import pallas as pl
from jax.experimental.pallas import tpu as pltpu
from jax.sharding import PartitionSpec as P

HEADS = 16
HD = 72
ROWS = 80
SCALE = HD**-0.5
LOG2E = 1.4426950408889634
VMEM_BYTES = 60 * 2**20
BF = jnp.bfloat16
F32 = jnp.float32
ALL = ("frame", "space")


def kernel_call(body, out_shape, scratch_shapes, flops, moved, args):
    return pl.pallas_call(
        body,
        out_shape=out_shape,
        scratch_shapes=scratch_shapes,
        compiler_params=pltpu.CompilerParams(vmem_limit_bytes=VMEM_BYTES),
        cost_estimate=pl.CostEstimate(flops=flops, bytes_accessed=moved, transcendentals=0),
    )(*args)


def shape(dims, dtype):
    return jax.ShapeDtypeStruct(dims, dtype)


def dot(a, b):
    return jnp.dot(a, b, preferred_element_type=F32)


def dot_nt(a, b):
    return lax.dot_general(a, b, (((1,), (1,)), ((), ())), preferred_element_type=F32)


def dot_tn(a, b):
    return lax.dot_general(a, b, (((0,), (0,)), ((), ())), preferred_element_type=F32)


def two_parts(x):
    high = x.astype(BF)
    return [high, (x - high.astype(F32)).astype(BF)]


def three_parts_rows(x, rows):
    high = x.astype(BF).astype(F32)
    rest = x - high
    mid = rest.astype(BF).astype(F32)
    low = rest - mid
    at = lax.broadcasted_iota(jnp.int32, (rows, x.shape[1]), 0)
    return jnp.where(at == 0, high, jnp.where(at == 1, mid, jnp.where(at == 2, low, 0.0))).astype(BF)


def minus_rows(rows, columns):
    at = lax.broadcasted_iota(jnp.int32, (rows, columns), 0)
    return jnp.where(at < 3, -1.0, 0.0).astype(BF)


def split_heads_body(q_ref, k_ref, v_ref, out_ref):
    tokens = q_ref.shape[1]
    at = lax.broadcasted_iota(jnp.int32, (ROWS - HD, tokens), 0)
    ones_row = jnp.where(at == 0, 1.0, 0.0)
    for i, ref in enumerate((q_ref, k_ref, v_ref)):
        flipped = ref[0].astype(F32).T
        for h in range(HEADS):
            fill = ones_row if i == 2 else jnp.zeros_like(ones_row)
            block = jnp.concatenate([flipped[h * HD : (h + 1) * HD], fill], axis=0)
            out_ref[h, i] = block.astype(BF)


def split_heads(query, key_rows, value_rows):
    tokens, width = query.shape[1:]
    return kernel_call(
        split_heads_body,
        shape((HEADS, 3, ROWS, tokens), BF),
        [],
        0,
        3 * tokens * width * 5,
        (query, key_rows, value_rows),
    )


def join_heads_body(in_ref, q_ref, k_ref, v_ref):
    for i, ref in enumerate((q_ref, k_ref, v_ref)):
        blocks = [in_ref[h, i].astype(F32)[:HD] for h in range(HEADS)]
        ref[0] = jnp.concatenate(blocks, axis=0).T.astype(BF)


def join_heads(blocks):
    tokens = blocks.shape[3]
    rows = shape((1, tokens, HEADS * HD), BF)
    return kernel_call(
        join_heads_body, (rows, rows, rows), [], 0, 3 * tokens * HEADS * HD * 5, (blocks,)
    )


def scaled_query(block):
    return two_parts(block.astype(F32) * (SCALE * LOG2E))


def space_forward_body(x_ref, o_ref, o_rows_ref, lse_ref, k_nat, v_rows):
    blocks, _, _, width = x_ref.shape

    def prepare(j, _):
        at = pl.ds(pl.multiple_of(j * width, width), width)
        k_block = x_ref[j, 1]
        k_nat[at, :] = jnp.concatenate([k_block, k_block], axis=0).T
        v_rows[:, at] = x_ref[j, 2]
        return 0

    lax.fori_loop(0, blocks, prepare, 0)

    def step(j, _):
        q_block = jnp.concatenate(scaled_query(x_ref[j, 0]), axis=0)
        scores = dot(k_nat[...], q_block)
        top = jnp.max(scores, axis=0, keepdims=True)
        probs = jnp.exp2(scores - top).astype(BF)
        mixed = dot(v_rows[...], probs)
        total = mixed[HD : HD + 1]
        mixed = mixed / total
        o_rows_ref[j] = mixed
        lse_ref[j] = jnp.broadcast_to(top + jnp.log2(total), (8, width))
        filled = jnp.concatenate([mixed[:HD], jnp.zeros((128 - HD, width), F32)], axis=0)
        o_ref[:, j] = filled.T.astype(BF).reshape(o_ref.shape[0], o_ref.shape[2], 128)
        return 0

    lax.fori_loop(0, blocks, step, 0)


def space_forward(blocks, frames):
    count, _, _, width = blocks.shape
    seq = count * width
    return kernel_call(
        space_forward_body,
        (
            shape((frames, count, width // frames, 128), BF),
            shape((count, ROWS, width), F32),
            shape((count, 8, width), F32),
        ),
        [pltpu.VMEM((seq, 2 * ROWS), BF), pltpu.VMEM((ROWS, seq), BF)],
        4 * seq * seq * 128,
        5 * 2**20,
        (blocks,),
    )


K_STEP = 256
Q_STEP = 1024


def space_backward_body(
    x_ref, o_rows_ref, lse_ref, g_ref, out_ref, q_aug, g_aug, q_rows, g_rows, p_buf, ds_buf, dq_sum
):
    blocks, _, _, width = x_ref.shape
    seq = blocks * width

    def prepare(j, _):
        at = pl.ds(pl.multiple_of(j * width, width), width)
        q_block = x_ref[j, 0]
        parts = scaled_query(q_block) + [three_parts_rows(lse_ref[j][:1], 16)]
        q_aug[at, :] = jnp.concatenate(parts, axis=0).T
        q_rows[:, at] = q_block
        g_block = g_ref[:, j].reshape(width, 128).astype(F32).T[:ROWS]
        inner = jnp.sum(g_block[:HD] * o_rows_ref[j][:HD], axis=0, keepdims=True)
        g_bf = g_block.astype(BF)
        g_rows[:, at] = g_bf
        g_aug[at, :] = jnp.concatenate([g_bf, three_parts_rows(inner, 16)], axis=0).T
        dq_sum[at, :] = jnp.zeros((width, ROWS), F32)
        return 0

    lax.fori_loop(0, blocks, prepare, 0)

    def step(j, _):
        k_block = x_ref[j, 1]
        v_block = x_ref[j, 2]
        k_aug = jnp.concatenate([k_block, k_block, minus_rows(16, width)], axis=0)
        v_aug = jnp.concatenate([v_block, minus_rows(16, width)], axis=0)
        k_nat = k_block.T

        for c in range(seq // Q_STEP):
            at = pl.ds(c * Q_STEP, Q_STEP)
            probs = jnp.exp2(dot(q_aug[at, :], k_aug))
            p_buf[at, :] = probs.astype(BF)
            ds = (probs * dot(g_aug[at, :], v_aug)).astype(BF)
            ds_buf[at, :] = ds
            dq_sum[at, :] += dot(ds, k_nat)

        out_ref[j, 1] = (dot(q_rows[...], ds_buf[...]) * SCALE).astype(BF)
        out_ref[j, 2] = dot(g_rows[...], p_buf[...]).astype(BF)
        return 0

    lax.fori_loop(0, blocks, step, 0)

    def finish(j, _):
        at = pl.ds(pl.multiple_of(j * width, width), width)
        out_ref[j, 0] = (dq_sum[at, :] * SCALE).T.astype(BF)
        return 0

    lax.fori_loop(0, blocks, finish, 0)


def space_backward(blocks, o_rows, lse, grads):
    count, _, _, width = blocks.shape
    seq = count * width
    return kernel_call(
        space_backward_body,
        shape(blocks.shape, BF),
        [
            pltpu.VMEM((seq, 2 * ROWS + 16), BF),
            pltpu.VMEM((seq, ROWS + 16), BF),
            pltpu.VMEM((ROWS, seq), BF),
            pltpu.VMEM((ROWS, seq), BF),
            pltpu.VMEM((seq, width), BF),
            pltpu.VMEM((seq, width), BF),
            pltpu.VMEM((seq, ROWS), F32),
        ],
        10 * seq * seq * 128,
        8 * 2**20,
        (blocks, o_rows, lse, grads),
    )


def middle_body(
    attn_ref,
    hidden_in_ref,
    cot_ref,
    w_space_ref,
    w_qkv_ref,
    w_time_ref,
    g_out_ref,
    gh_ref,
    attn_space_ref,
    hidden_ref,
    attn_time_ref,
    dqkv_ref,
    qkv_ref,
    ga_ref,
):
    frames, _, positions, _ = attn_ref.shape
    tokens = frames * positions
    width = HEADS * HD
    for h in range(HEADS):
        block = attn_ref[:, h].reshape(tokens, 128)
        attn_space_ref[:, h * HD : (h + 1) * HD] = block[:, :HD]
    cot = cot_ref[...].reshape(tokens, width)
    base = hidden_in_ref[...].reshape(tokens, width).astype(F32)
    hidden_ref[...] = (base + dot(attn_space_ref[...], w_space_ref[...])).astype(BF)
    for c in range(3):
        at = pl.ds(c * width, width)
        qkv_ref[:, at] = dot(hidden_ref[...], w_qkv_ref[:, at]).astype(BF)
    ga_ref[...] = dot_nt(cot, w_time_ref[...]).astype(BF)

    same = (
        lax.broadcasted_iota(jnp.int32, (tokens, tokens), 0) % positions
        == lax.broadcasted_iota(jnp.int32, (tokens, tokens), 1) % positions
    )
    for h in range(HEADS):
        lo, hi = h * HD, (h + 1) * HD
        q = qkv_ref[:, lo:hi]
        k = qkv_ref[:, width + lo : width + hi]
        v = qkv_ref[:, 2 * width + lo : 2 * width + hi]
        g = ga_ref[:, lo:hi]
        scores = jnp.where(same, dot_nt(q, k) * SCALE, -jnp.inf)
        exps = jnp.exp(scores - jnp.max(scores, axis=1, keepdims=True))
        probs = exps / jnp.sum(exps, axis=1, keepdims=True)
        probs_bf = probs.astype(BF)
        attn_time_ref[:, lo:hi] = dot(probs_bf, v).astype(BF)
        weighted = probs * dot_nt(g, v)
        ds = ((weighted - probs * jnp.sum(weighted, axis=1, keepdims=True)) * SCALE).astype(BF)
        dqkv_ref[:, lo:hi] = dot(ds, k).astype(BF)
        dqkv_ref[:, width + lo : width + hi] = dot_tn(ds, q).astype(BF)
        dqkv_ref[:, 2 * width + lo : 2 * width + hi] = dot_tn(probs_bf, g).astype(BF)

    gh_ref[...] = (cot.astype(F32) + dot_nt(dqkv_ref[...], w_qkv_ref[...])).astype(BF)
    ga_ref[...] = dot_nt(gh_ref[...], w_space_ref[...]).astype(BF)
    for h in range(HEADS):
        block = ga_ref[:, h * HD : (h + 1) * HD]
        filled = jnp.concatenate([block, jnp.zeros((tokens, 128 - HD), BF)], axis=1)
        g_out_ref[:, h] = filled.reshape(frames, positions, 128)


def middle(attn, hidden_in, cot, w_space_out, w_time_qkv, w_time_out):
    frames, _, positions, _ = attn.shape
    tokens = frames * positions
    width = HEADS * HD
    rows = shape((tokens, width), BF)
    wide = shape((tokens, 3 * width), BF)
    return kernel_call(
        middle_body,
        (shape(attn.shape, BF), rows, rows, rows, rows, wide),
        [pltpu.VMEM((tokens, 3 * width), BF), pltpu.VMEM((tokens, width), BF)],
        2 * tokens * width * width * 9,
        20 * 2**20,
        (attn, hidden_in, cot, w_space_out, w_time_qkv, w_time_out),
    )


def exchange(blocks, axis):
    return lax.all_to_all(blocks, axis, split_axis=0, concat_axis=0, tiled=True)


def exchange_all(blocks):
    flat = exchange(blocks.reshape((-1,) + blocks.shape[2:]), ALL)
    return flat.reshape(blocks.shape)


def grad_terms(rows, grads):
    return lax.dot_general(rows, grads, (((0,), (0,)), ((), ())), preferred_element_type=F32)


def shards(
    hidden_in, query_space, key_space, value_space, cotangent, w_space_out, w_time_qkv, w_time_out
):
    tile_rows, width = hidden_in.shape[1:]
    frames = lax.axis_size("frame")
    positions = tile_rows // frames
    by_frame = (frames, positions, width)

    head_blocks = exchange(split_heads(query_space, key_space, value_space), "space")
    hidden_cols = exchange(hidden_in.reshape(by_frame), "frame")
    cot_cols = exchange(cotangent.reshape(by_frame), "frame")
    mixed, o_rows, lse = space_forward(head_blocks, frames)
    attn = exchange_all(mixed)
    g_out, grad_cols, attn_space, hidden, attn_time, dqkv = middle(
        attn, hidden_cols, cot_cols, w_space_out, w_time_qkv, w_time_out
    )
    grads = exchange_all(g_out)
    cot = cot_cols.reshape(-1, width)
    sums = [
        lax.psum_scatter(terms, ALL, scatter_dimension=0, tiled=True)
        for terms in (
            grad_terms(attn_space, grad_cols),
            grad_terms(hidden, dqkv),
            grad_terms(attn_time, cot),
        )
    ]
    out_cols = (
        hidden.astype(F32) + jnp.dot(attn_time, w_time_out, preferred_element_type=F32)
    ).astype(BF)
    block_out = exchange(out_cols.reshape(by_frame), "frame").reshape(hidden_in.shape)
    grad_hidden = exchange(grad_cols.reshape(by_frame), "frame").reshape(hidden_in.shape)
    back = exchange(space_backward(head_blocks, o_rows, lse, grads), "space")
    return (block_out, grad_hidden, *join_heads(back), *sums)


def solution(mesh):
    rows = P("frame", "space", None)
    weights = P(ALL, None)
    return jax.shard_map(
        shards,
        mesh=mesh,
        in_specs=(rows,) * 5 + (P(),) * 3,
        out_specs=(rows,) * 5 + (weights,) * 3,
        check_vma=False,
    )
```

time: 743 us -> 446 us (0.60); the launches traced: 730 us -> 445 us
  matrix products: 251 us -> 18.7 us
  local copies, waits for them, and re-layouts: 185 us -> 6.3 us
  other arithmetic: 140 us -> 0 us
  Pallas kernels: 0 us -> 121 us
  blocking collectives: 0 us -> 106 us
  waiting for transfers between devices: 85.8 us -> 159 us
  starting transfers between devices: 52.8 us -> 19.8 us
    dot_general x71 -> x4, matrix products: 251 us -> 18.7 us  [the longest x3 15.9 us: grad_terms(): lax.dot_general(rows, grads, (((0,), (0,)), ((), ())), preferred_element_...]
    unnamed x2, waiting for transfers between devices: 0.02 us -> 123 us
    pallas_call x0 -> x5, Pallas kernels: none -> 121 us  [kernel_call(): pl.pallas_call(body, out_shape=out_shape, scratch_shapes=scratch_shapes,...]
    all_to_all x0 -> x4, blocking collectives: none -> 106 us  [exchange(): return lax.all_to_all(blocks, axis, split_axis=0, concat_axis=0, tiled=True)]
    convert_element_type x8 -> x0, other arithmetic: 85.1 us -> none  [backward_step(): (probs * (grad_probs - row_inner) * score_scale).astype(jnp.bfloat16)]
    unnamed x56 -> x20, local copies, waits for them, and re-layouts: 63.7 us -> 6.3 us
    all_to_all x8 -> x4, waiting for transfers between devices: 85.8 us -> 36.2 us  [exchange(): return lax.all_to_all(blocks, axis, split_axis=0, concat_axis=0, tiled=True)]
    unnamed x5 -> x0, other arithmetic: 36.7 us -> none
  transfers between devices with their start and end apart: 9 -> 5, of which waited for: 5 -> 3; matrix products, arithmetic and copies ran while one was open for 54% -> 1% of each run, Pallas kernels for 0% -> 21%
where the time goes in v1:
time: 446 us; the launch traced here: 445 us
  waiting for transfers between devices  159 us (36%)
  Pallas kernels  121 us (27%)
  blocking collectives  106 us (24%)
  starting transfers between devices  19.8 us (4%)
  matrix products  18.7 us (4%)
  between operations  14.1 us (3%)
  local copies, waits for them, and re-layouts  6.3 us (1%)
    unnamed x2, waiting for transfers between devices  123 us
    pallas_call x5, Pallas kernels, kernel_call(): pl.pallas_call(body, out_shape=out_shape, scratch_shapes=scratch_shapes,...  121 us
    all_to_all x4, blocking collectives, exchange(): return lax.all_to_all(blocks, axis, split_axis=0, concat_axis=0, tiled=True)  106 us
    all_to_all x4, waiting for transfers between devices, exchange(): return lax.all_to_all(blocks, axis, split_axis=0, concat_axis=0, tiled=True)  36.2 us
    all_to_all x4, starting transfers between devices, exchange(): return lax.all_to_all(blocks, axis, split_axis=0, concat_axis=0, tiled=True)  19.8 us
    dot_general x3, matrix products, grad_terms(): lax.dot_general(rows, grads, (((0,), (0,)), ((), ())), preferred_element_...  15.9 us
  transfers between devices with their start and end apart: 5, of which 3 were waited for; matrix products, arithmetic and copies ran while one was open for 1% of the time, Pallas kernels for 21%

profile of v1, /device:TPU:1, one launch (start us, length us, event | category | flops | bytes accessed | tf_op | source)
XLA Modules:
  0.0 444.9 jit_solution(3055529892377721594)
XLA Ops:
  7.2 6.9 %all-to-all-start.2 = ((bf16[8,32,1152]{2,1,0:T(8,128)(2,1)}), bf16[8,32,1152]{2,1,0:T(8,128)(2,1)S(1)}, u32[]{:S(2)}, u32[]{:S(2)}) async-start(bf16[8,32,1152]{2,1,0:T(8,128)(2,1)} %bitcast.26), calls=%async_computation.2 | async-start | bytes 1179648 | tf_op jit(solution)/shard_map/all_to_all | solution.py:304
  14.1 3.3 shard_map.143
  17.3 6.6 %all-to-all-done.2.hidden_in_ref = bf16[8,32,1152]{2,1,0:T(8,128)(2,1)S(1)} async-done(((bf16[8,32,1152]{2,1,0:T(8,128)(2,1)}), bf16[8,32,1152]{2,1,0:T(8,128)(2,1)S(1)}, u32[]{:S(2)}, u32[]{:S(2)}) %all-to-all-start.2) | async-done | bytes 589856 | tf_op jit(solution)/shard_map/all_to_all | solution.py:304
  23.9 35.5 %all_to_all.40.x_ref = bf16[16,3,80,256]{3,2,1,0:T(8,128)(2,1)} all-to-all(bf16[16,3,80,256]{3,2,1,0:T(8,128)(2,1)} %shard_map.143), channel_id=1, replica_groups=mesh['frame'=8,'space'=16] {'space'}, dimensions={0} | all-to-all | bytes 3932160 | tf_op jit(solution)/shard_map/all_to_all | solution.py:304
  59.5 3.5 all-to-all-start.3
  63.0 0.0 all-reduce.6.cloned.1.call-start
  63.1 40.5 %shard_map.144 = (bf16[8,16,32,128]{3,2,1,0:T(8,128)(2,1)}, f32[16,80,256]{2,1,0:T(8,128)}, f32[16,8,256]{2,1,0:T(8,128)}) custom-call(bf16[16,3,80,256]{3,2,1,0:T(8,128)(2,1)} %all_to_all.40.x_ref), custom_call_target="tpu_custom_call" | custom-call | flops 8589934592 | bytes 5242880 | tf_op jit(solution)/shard_map/pallas_call | solution.py:20
  103.5 0.0 all-to-all-done.3.cot_ref
  103.6 25.5 %all_to_all.41 = bf16[128,32,128]{2,1,0:T(8,128)(2,1)} all-to-all(bf16[128,32,128]{2,1,0:T(8,128)(2,1)} %bitcast.25), channel_id=1, replica_groups=mesh['frame'=8,'space'=16] {'frame','space'}, dimensions={0} | all-to-all | bytes 2097152 | tf_op jit(solution)/shard_map/all_to_all | solution.py:304
  129.0 0.0 copy-done.1
  129.0 27.0 %shard_map.145 = (bf16[8,16,32,128]{3,2,1,0:T(8,128)(2,1)}, bf16[256,1152]{1,0:T(8,128)(2,1)}, bf16[256,1152]{1,0:T(8,128)(2,1)}, bf16[256,1152]{1,0:T(8,128)(2,...) custom-call(bf16[8,16,32,128]{3,2,1,0:T(8,128)(2,1)} %bitcast.24, bf16[8,32,1152]{2,1,0:T(8,128)(2,1)} %copy-done.7, ...), custom_call_target="tpu_custom_call" | custom-call | flops 6115295232 | bytes 20971520 | tf_op jit(solution)/shard_map/pallas_call | solution.py:20
  156.1 0.0 copy-start.6
  156.1 4.8 %fusion.1 = f32[1152,1152]{1,0:T(8,128)} fusion(bf16[256,1152]{1,0:T(8,128)(2,1)} %get-tuple-element.30, bf16[256,1152]{1,0:T(8,128)(2,1)} %get-tuple-element.23), kind=kOutput, calls=%fused_computation.5 | convolution fusion | flops 679477248 | bytes 6488064 | tf_op jit(solution)/shard_map/dot_general | solution.py:313
  160.9 7.8 %fusion.2 = f32[1152,3456]{1,0:T(8,128)} fusion(bf16[256,1152]{1,0:T(8,128)(2,1)S(1)} %copy-done.6, bf16[256,3456]{1,0:T(8,128)(2,1)S(1)} %copy-done.3), kind=kOutput, calls=%fused_computation.6 | convolution fusion | flops 2038431744 | bytes 18284544 | tf_op jit(solution)/shard_map/dot_general | solution.py:313
  168.7 0.0 copy-done.2
  168.7 3.3 fusion.3
  172.0 0.0 all-reduce.6.cloned.1.call-update
  172.0 2.8 fusion
  174.8 15.6 %all_to_all.42 = bf16[8,32,1152]{2,1,0:T(8,128)(2,1)S(1)} all-to-all(bf16[8,32,1152]{2,1,0:T(8,128)(2,1)S(1)} %bitcast.27), channel_id=1, replica_groups=mesh['frame'=8,'space'=16] {'frame'}, dimensions={0} | all-to-all | bytes 1179648 | tf_op jit(solution)/shard_map/all_to_all | solution.py:304
  190.5 28.9 %all_to_all.43 = bf16[128,32,128]{2,1,0:T(8,128)(2,1)} all-to-all(bf16[128,32,128]{2,1,0:T(8,128)(2,1)S(1)} %bitcast.22), channel_id=1, replica_groups=mesh['frame'=8,'space'=16] {'frame','space'}, dimensions={0} | all-to-all | bytes 2097152 | tf_op jit(solution)/shard_map/all_to_all | solution.py:304
  219.4 3.8 all-to-all-start.5
  223.2 47.7 %shard_map.146 = bf16[16,3,80,256]{3,2,1,0:T(8,128)(2,1)} custom-call(bf16[16,3,80,256]{3,2,1,0:T(8,128)(2,1)} %all_to_all.40.x_ref, f32[16,80,256]{2,1,0:T(8,128)} %get-tuple-element.24.o_rows_ref, f32[16,8,256]{2,1,0:T(8,128)} %get-tuple-element.25.lse_ref, bf16[8,16,32,128]{3,2,1,0:T(8,128)(2,1)} %bitcast.23), custom_call_target="tpu_custom_call" | custom-call | flops 21474836480 | bytes 8388608 | tf_op jit(solution)/shard_map/pallas_call | solution.py:20
  270.9 0.0 all-to-all-done.5
  270.9 5.6 %all-to-all-start.7 = ((bf16[16,3,80,256]{3,2,1,0:T(8,128)(2,1)}), bf16[16,3,80,256]{3,2,1,0:T(8,128)(2,1)S(1)}, u32[]{:S(2)}, u32[]{:S(2)}) async-start(bf16[16,3,80,256]{3,2,1,0:T(8,128)(2,1)} %shard_map.146), calls=%async_computation.7 | async-start | bytes 3932160 | tf_op jit(solution)/shard_map/all_to_all | solution.py:304
  276.5 29.6 %all-to-all-done.7.in_ref = bf16[16,3,80,256]{3,2,1,0:T(8,128)(2,1)S(1)} async-done(((bf16[16,3,80,256]{3,2,1,0:T(8,128)(2,1)}), bf16[16,3,80,256]{3,2,1,0:T(8,128)(2,1)S(1)}, u32[]{:S(2)}, u32[]{:S(2)}) %all-to-all-start.7) | async-done | bytes 1966112 | tf_op jit(solution)/shard_map/all_to_all | solution.py:304
  306.1 1.3 copy-done
  307.4 3.0 shard_map.147
  310.4 122.7 %all-reduce.6.cloned.1.call-done = (f32[1152,1152]{1,0:T(8,128)}, f32[1152,3456]{1,0:T(8,128)}, f32[1152,1152]{1,0:T(8,128)}) async-done(((f32[1152,1152]{1,0:T(8,128)}, f32[1152,3456]{1,0:T(8,128)}, f32[1152,1152]{1,0:T(8,128)}), (f32[1152,1152]{1,0:T(8,128)}, f32[1152,3456]{1,0:T(8,128)}, f32[1152,1152]{1,0:T(8,128)})) %all-reduce.6.cloned.1.call-update) | async-done | bytes 26542096
  433.1 1.7 constant_dynamic-slice_fusion.1
  434.8 1.6 constant_dynamic-slice_fusion
  436.4 0.8 copy.21
  437.2 0.8 copy.22
  (12 shorter events, 0.0 us)
Async XLA Ops:
  7.2 16.8 %all-to-all-start.2 = ((bf16[8,32,1152]{2,1,0:T(8,128)(2,1)}), bf16[8,32,1152]{2,1,0:T(8,128)(2,1)S(1)}, u32[]{:S(2)}, u32[]{:S(2)}) async-start(bf16[8,32,1152]{2,1,0:T(8,128)(2,1)} %bitcast.26), calls=%async_computation.2 | async-start | bytes 1179648 | tf_op jit(solution)/shard_map/all_to_all | solution.py:304
  23.9 79.6 %copy-start.7 = (bf16[8,32,1152]{2,1,0:T(8,128)(2,1)}, bf16[8,32,1152]{2,1,0:T(8,128)(2,1)S(1)}, u32[]{:S(2)}) copy-start(bf16[8,32,1152]{2,1,0:T(8,128)(2,1)S(1)} %all-to-all-done.2.hidden_in_ref) | copy-start | bytes 1769476
  59.5 44.1 %all-to-all-start.3 = ((bf16[8,32,1152]{2,1,0:T(8,128)(2,1)}), bf16[8,32,1152]{2,1,0:T(8,128)(2,1)S(1)}, u32[]{:S(2)}, u32[]{:S(2)}) async-start(bf16[8,32,1152]{2,1,0:T(8,128)(2,1)} %bitcast.3), calls=%async_computation.3 | async-start | bytes 1179648 | tf_op jit(solution)/shard_map/all_to_all | solution.py:304
  63.0 370.1 %all-reduce.6.cloned.1.call-start = ((), (), s32[]{:S(2)}) async-start(), calls=%async_computation.8 | async-start | bytes 53084160
  103.5 25.5 %copy-start.1 = (bf16[8,32,1152]{2,1,0:T(8,128)(2,1)}, bf16[8,32,1152]{2,1,0:T(8,128)(2,1)S(1)}, u32[]{:S(2)}) copy-start(bf16[8,32,1152]{2,1,0:T(8,128)(2,1)S(1)} %all-to-all-done.3.cot_ref) | copy-start | bytes 1769476
  156.1 4.8 %copy-start.3 = (bf16[256,3456]{1,0:T(8,128)(2,1)S(1)}, bf16[256,3456]{1,0:T(8,128)(2,1)}, u32[]{:S(2)}) copy-start(bf16[256,3456]{1,0:T(8,128)(2,1)} %get-tuple-element.31) | copy-start | bytes 5308420
  156.1 4.8 %copy-start.6 = (bf16[256,1152]{1,0:T(8,128)(2,1)S(1)}, bf16[256,1152]{1,0:T(8,128)(2,1)}, u32[]{:S(2)}) copy-start(bf16[256,1152]{1,0:T(8,128)(2,1)} %get-tuple-element.21) | copy-start | bytes 1769476
  160.9 7.9 %copy-start.2 = (bf16[8,32,1152]{2,1,0:T(8,128)(2,1)S(1)}, bf16[8,32,1152]{2,1,0:T(8,128)(2,1)}, u32[]{:S(2)}) copy-start(bf16[8,32,1152]{2,1,0:T(8,128)(2,1)} %copy-done.1) | copy-start | bytes 1769476
  160.9 7.9 %copy-start.4 = (bf16[256,1152]{1,0:T(8,128)(2,1)S(1)}, bf16[256,1152]{1,0:T(8,128)(2,1)}, u32[]{:S(2)}) copy-start(bf16[256,1152]{1,0:T(8,128)(2,1)} %get-tuple-element.22) | copy-start | bytes 1769476
  172.0 18.5 %copy-start.5 = (bf16[8,16,32,128]{3,2,1,0:T(8,128)(2,1)S(1)}, bf16[8,16,32,128]{3,2,1,0:T(8,128)(2,1)}, u32[]{:S(2)}) copy-start(bf16[8,16,32,128]{3,2,1,0:T(8,128)(2,1)} %get-tuple-element.26) | copy-start | bytes 3145732
  219.4 51.5 %all-to-all-start.5 = ((bf16[8,32,1152]{2,1,0:T(8,128)(2,1)}), bf16[8,32,1152]{2,1,0:T(8,128)(2,1)S(1)}, u32[]{:S(2)}, u32[]{:S(2)}) async-start(bf16[8,32,1152]{2,1,0:T(8,128)(2,1)} %bitcast.6), calls=%async_computation.5 | async-start | bytes 1179648 | tf_op jit(solution)/shard_map/all_to_all | solution.py:304
  270.9 35.1 %all-to-all-start.7 = ((bf16[16,3,80,256]{3,2,1,0:T(8,128)(2,1)}), bf16[16,3,80,256]{3,2,1,0:T(8,128)(2,1)S(1)}, u32[]{:S(2)}, u32[]{:S(2)}) async-start(bf16[16,3,80,256]{3,2,1,0:T(8,128)(2,1)} %shard_map.146), calls=%async_computation.7 | async-start | bytes 3932160 | tf_op jit(solution)/shard_map/all_to_all | solution.py:304
  306.1 1.3 copy-start
Sparse Core Ops, SparseCore 0:
  172.1 260.9 all-reduce.5

commit v2 on v1

--- a/solution.py
+++ b/solution.py
@@ -10,7 +10,7 @@
 ROWS = 80
 SCALE = HD**-0.5
 LOG2E = 1.4426950408889634
-VMEM_BYTES = 60 * 2**20
+VMEM_BYTES = 62 * 2**20
 BF = jnp.bfloat16
 F32 = jnp.float32
 ALL = ("frame", "space")
@@ -149,15 +149,13 @@
     )
 
 
-K_STEP = 256
 Q_STEP = 1024
-
-
-def space_backward_body(
-    x_ref, o_rows_ref, lse_ref, g_ref, out_ref, q_aug, g_aug, q_rows, g_rows, p_buf, ds_buf, dq_sum
-):
+TILE_ROWS = 144
+TILE_COLS = 384
+
+
+def backward_prepare(x_ref, o_rows_ref, lse_ref, g_ref, q_aug, g_aug, q_rows, g_rows, dq_sum):
     blocks, _, _, width = x_ref.shape
-    seq = blocks * width
 
     def prepare(j, _):
         at = pl.ds(pl.multiple_of(j * width, width), width)
@@ -175,6 +173,13 @@
 
     lax.fori_loop(0, blocks, prepare, 0)
 
+
+def backward_steps(
+    first, last, x_ref, out_ref, q_aug, g_aug, q_rows, g_rows, p_buf, ds_buf, dq_sum
+):
+    blocks, _, _, width = x_ref.shape
+    seq = blocks * width
+
     def step(j, _):
         k_block = x_ref[j, 1]
         v_block = x_ref[j, 2]
@@ -194,7 +199,11 @@
         out_ref[j, 2] = dot(g_rows[...], p_buf[...]).astype(BF)
         return 0
 
-    lax.fori_loop(0, blocks, step, 0)
+    lax.fori_loop(first, last, step, 0)
+
+
+def backward_finish(out_ref, dq_sum):
+    blocks, _, _, width = out_ref.shape
 
     def finish(j, _):
         at = pl.ds(pl.multiple_of(j * width, width), width)
@@ -204,13 +213,235 @@
     lax.fori_loop(0, blocks, finish, 0)
 
 
-def space_backward(blocks, o_rows, lse, grads):
+def add_into(target, terms, lead):
+    count = 1
+    for n in lead:
+        count *= n
+
+    def one(i, _):
+        index = []
+        for n in reversed(lead):
+            index.insert(0, lax.rem(i, n))
+            i = lax.div(i, n)
+        total = target(*index)[...].astype(F32)
+        for term in terms:
+            total = total + term(*index)[...].astype(F32)
+        target(*index)[...] = total.astype(BF)
+        return 0
+
+    lax.fori_loop(0, count, one, 0)
+
+
+def space_backward_body(
+    x_ref,
+    o_rows_ref,
+    lse_ref,
+    g_ref,
+    attn_space_ref,
+    hidden_ref,
+    attn_time_ref,
+    gh_ref,
+    dqkv_ref,
+    cot_ref,
+    out_ref,
+    sums_ref,
+    q_aug,
+    g_aug,
+    q_rows,
+    g_rows,
+    p_buf,
+    ds_buf,
+    dq_sum,
+    terms,
+    half,
+    x_in_a,
+    z_in_b,
+    z_in_a,
+    x_in_b,
+    lo_in,
+    hi_in,
+    mine,
+    gathered,
+    send1,
+    recv1,
+    send2,
+    recv2,
+    send3,
+    recv3,
+    send4,
+    recv4,
+    send6,
+    recv6,
+):
+    frame, space = lax.axis_index("frame"), lax.axis_index("space")
+    z, lo = lax.div(frame, 2), lax.rem(frame, 2)
+    x, hi, core = lax.div(space, 4), lax.rem(lax.div(space, 2), 2), lax.rem(space, 2)
+
+    def x_peer(i):
+        return (frame, lax.rem(x + i, 4) * 4 + hi * 2 + core)
+
+    def z_peer(i):
+        return (lax.rem(z + i, 4) * 2 + lo, space)
+
+    def space_peer(i):
+        return (frame, lax.rem(space + i, 16))
+
+    lo_peer = (z * 2 + 1 - lo, space)
+    hi_peer = (frame, x * 4 + (1 - hi) * 2 + core)
+    core_peer = (frame, x * 4 + hi * 2 + 1 - core)
+
+    def copy(src, dst, send_sem, recv_sem, device):
+        return pltpu.make_async_remote_copy(
+            src_ref=src,
+            dst_ref=dst,
+            send_sem=send_sem,
+            recv_sem=recv_sem,
+            device_id=device,
+            device_id_type=pl.DeviceIdType.MESH,
+        )
+
+    barrier = pltpu.get_barrier_semaphore()
+    peers = [space_peer(i) for i in range(1, 16)] + [z_peer(i) for i in range(1, 4)] + [lo_peer]
+    for peer in peers:
+        pl.semaphore_signal(barrier, inc=1, device_id=peer, device_id_type=pl.DeviceIdType.MESH)
+
+    for t, (rows_ref, grads_ref, offset) in enumerate(
+        [(attn_space_ref, gh_ref, c) for c in range(3)]
+        + [(hidden_ref, dqkv_ref, c) for c in range(9)]
+        + [(attn_time_ref, cot_ref, c) for c in range(3)]
+    ):
+        part = dot_tn(rows_ref[...], grads_ref[:, offset * TILE_COLS : (offset + 1) * TILE_COLS])
+        part = part.astype(BF)
+        for f in range(8):
+            rows = part[f * TILE_ROWS : (f + 1) * TILE_ROWS]
+            terms[f % 2, f // 2, t // 4, t // 2 % 2, t % 2] = rows
+    for f in range(8):
+        terms[f % 2, f // 2, 3, 1, 1] = jnp.zeros((TILE_ROWS, TILE_COLS), BF)
+
+    pl.semaphore_wait(barrier, len(peers))
+
+    first = [
+        copy(
+            terms.at[y, w, :, :, 1 - core],
+            half.at[y, w],
+            send1.at[y, w],
+            recv1.at[y, w],
+            core_peer,
+        )
+        for y in range(2)
+        for w in range(4)
+    ]
+    for c in first:
+        c.start()
+
+    state = (q_aug, g_aug, q_rows, g_rows)
+    backward_prepare(x_ref, o_rows_ref, lse_ref, g_ref, *state, dq_sum)
+
+    def attend(start, stop):
+        backward_steps(start, stop, x_ref, out_ref, *state, p_buf, ds_buf, dq_sum)
+
+    attend(0, STAGES[0])
+
+    for c in first:
+        c.wait()
+    add_into(
+        lambda y, w, a, b: half.at[y, w, a, b],
+        [lambda y, w, a, b: terms.at[y, w, a, b, core]],
+        (2, 4, 4, 2),
+    )
+    second = []
+    for i in range(1, 4):
+        to_x, to_z = lax.rem(x + i, 4), lax.rem(z + i, 4)
+        s = i - 1
+        second.append(
+            copy(half.at[0, :, to_x], x_in_a.at[s], send2.at[0, s], recv2.at[0, s], x_peer(i))
+        )
+        second.append(
+            copy(half.at[1, to_z], z_in_b.at[s], send2.at[1, s], recv2.at[1, s], z_peer(i))
+        )
+    for c in second:
+        c.start()
+
+    attend(STAGES[0], STAGES[1])
+
+    for c in second:
+        c.wait()
+    add_into(
+        lambda w, b: half.at[0, w, x, b],
+        [lambda w, b, s=s: x_in_a.at[s, w, b] for s in range(3)],
+        (4, 2),
+    )
+    add_into(
+        lambda a, b: half.at[1, z, a, b],
+        [lambda a, b, s=s: z_in_b.at[s, a, b] for s in range(3)],
+        (4, 2),
+    )
+    third = []
+    for i in range(1, 4):
+        to_x, to_z = lax.rem(x + i, 4), lax.rem(z + i, 4)
+        s = i - 1
+        third.append(
+            copy(half.at[0, to_z, x], z_in_a.at[s], send3.at[0, s], recv3.at[0, s], z_peer(i))
+        )
+        third.append(
+            copy(half.at[1, z, to_x], x_in_b.at[s], send3.at[1, s], recv3.at[1, s], x_peer(i))
+        )
+    for c in third:
+        c.start()
+
+    attend(STAGES[1], STAGES[2])
+
+    for c in third:
+        c.wait()
+    add_into(
+        lambda b: half.at[0, z, x, b], [lambda b, s=s: z_in_a.at[s, b] for s in range(3)], (2,)
+    )
+    add_into(
+        lambda b: half.at[1, z, x, b], [lambda b, s=s: x_in_b.at[s, b] for s in range(3)], (2,)
+    )
+    fourth = copy(half.at[1 - lo, z, x], lo_in, send4.at[0], recv4.at[0], lo_peer)
+    fourth.start()
+
+    attend(STAGES[2], STAGES[3])
+
+    fourth.wait()
+    add_into(lambda b: half.at[lo, z, x, b], [lambda b: lo_in.at[b]], (2,))
+    fifth = copy(half.at[lo, z, x, 1 - hi], hi_in, send4.at[1], recv4.at[1], hi_peer)
+    fifth.start()
+
+    attend(STAGES[3], 16)
+
+    fifth.wait()
+    total = (half[lo, z, x, hi].astype(F32) + hi_in[...].astype(F32)).astype(BF)
+    mine[...] = total
+    sixth = [
+        copy(mine, gathered.at[i - 1], send6.at[i - 1], recv6.at[i - 1], space_peer(i))
+        for i in range(1, 16)
+    ]
+    for c in sixth:
+        c.start()
+
+    backward_finish(out_ref, dq_sum)
+    sums_ref[space] = total
+    for i, c in enumerate(sixth):
+        c.wait()
+        sums_ref[lax.rem(space + 15 - i, 16)] = gathered[i]
+
+
+STAGES = (3, 10, 13, 15)
+
+
+def space_backward(blocks, o_rows, lse, grads, pairs):
     count, _, _, width = blocks.shape
     seq = count * width
-    return kernel_call(
+    tile = (TILE_ROWS, TILE_COLS)
+    dma = pltpu.SemaphoreType.DMA
+    return pl.pallas_call(
         space_backward_body,
-        shape(blocks.shape, BF),
-        [
+        out_shape=(shape(blocks.shape, BF), shape((16,) + tile, BF)),
+        in_specs=[pl.BlockSpec(memory_space=pltpu.VMEM)] * 10,
+        out_specs=[pl.BlockSpec(memory_space=pltpu.VMEM)] * 2,
+        scratch_shapes=[
             pltpu.VMEM((seq, 2 * ROWS + 16), BF),
             pltpu.VMEM((seq, ROWS + 16), BF),
             pltpu.VMEM((ROWS, seq), BF),
@@ -218,11 +449,34 @@
             pltpu.VMEM((seq, width), BF),
             pltpu.VMEM((seq, width), BF),
             pltpu.VMEM((seq, ROWS), F32),
+            pltpu.VMEM((2, 4, 4, 2, 2) + tile, BF),
+            pltpu.VMEM((2, 4, 4, 2) + tile, BF),
+            pltpu.VMEM((3, 4, 2) + tile, BF),
+            pltpu.VMEM((3, 4, 2) + tile, BF),
+            pltpu.VMEM((3, 2) + tile, BF),
+            pltpu.VMEM((3, 2) + tile, BF),
+            pltpu.VMEM((2,) + tile, BF),
+            pltpu.VMEM(tile, BF),
+            pltpu.VMEM(tile, BF),
+            pltpu.VMEM((15,) + tile, BF),
+            dma((2, 4)),
+            dma((2, 4)),
+            dma((2, 3)),
+            dma((2, 3)),
+            dma((2, 3)),
+            dma((2, 3)),
+            dma((2,)),
+            dma((2,)),
+            dma((15,)),
+            dma((15,)),
         ],
-        10 * seq * seq * 128,
-        8 * 2**20,
-        (blocks, o_rows, lse, grads),
-    )
+        compiler_params=pltpu.CompilerParams(
+            vmem_limit_bytes=VMEM_BYTES, collective_id=0, has_side_effects=True
+        ),
+        cost_estimate=pl.CostEstimate(
+            flops=10 * seq * seq * 128, bytes_accessed=16 * 2**20, transcendentals=0
+        ),
+    )(blocks, o_rows, lse, grads, *pairs)
 
 
 def middle_body(
@@ -234,6 +488,7 @@
     w_time_ref,
     g_out_ref,
     gh_ref,
+    out_ref,
     attn_space_ref,
     hidden_ref,
     attn_time_ref,
@@ -282,6 +537,8 @@
         block = ga_ref[:, h * HD : (h + 1) * HD]
         filled = jnp.concatenate([block, jnp.zeros((tokens, 128 - HD), BF)], axis=1)
         g_out_ref[:, h] = filled.reshape(frames, positions, 128)
+    out = hidden_ref[...].astype(F32) + dot(attn_time_ref[...], w_time_ref[...])
+    out_ref[...] = out.astype(BF)
 
 
 def middle(attn, hidden_in, cot, w_space_out, w_time_qkv, w_time_out):
@@ -292,9 +549,9 @@
     wide = shape((tokens, 3 * width), BF)
     return kernel_call(
         middle_body,
-        (shape(attn.shape, BF), rows, rows, rows, rows, wide),
+        (shape(attn.shape, BF), rows, rows, rows, rows, rows, wide),
         [pltpu.VMEM((tokens, 3 * width), BF), pltpu.VMEM((tokens, width), BF)],
-        2 * tokens * width * width * 9,
+        2 * tokens * width * width * 10,
         20 * 2**20,
         (attn, hidden_in, cot, w_space_out, w_time_qkv, w_time_out),
     )
@@ -307,10 +564,6 @@
 def exchange_all(blocks):
     flat = exchange(blocks.reshape((-1,) + blocks.shape[2:]), ALL)
     return flat.reshape(blocks.shape)
-
-
-def grad_terms(rows, grads):
-    return lax.dot_general(rows, grads, (((0,), (0,)), ((), ())), preferred_element_type=F32)
 
 
 def shards(
@@ -326,26 +579,20 @@
     cot_cols = exchange(cotangent.reshape(by_frame), "frame")
     mixed, o_rows, lse = space_forward(head_blocks, frames)
     attn = exchange_all(mixed)
-    g_out, grad_cols, attn_space, hidden, attn_time, dqkv = middle(
+    g_out, grad_cols, out_cols, attn_space, hidden, attn_time, dqkv = middle(
         attn, hidden_cols, cot_cols, w_space_out, w_time_qkv, w_time_out
     )
     grads = exchange_all(g_out)
-    cot = cot_cols.reshape(-1, width)
-    sums = [
-        lax.psum_scatter(terms, ALL, scatter_dimension=0, tiled=True)
-        for terms in (
-            grad_terms(attn_space, grad_cols),
-            grad_terms(hidden, dqkv),
-            grad_terms(attn_time, cot),
-        )
-    ]
-    out_cols = (
-        hidden.astype(F32) + jnp.dot(attn_time, w_time_out, preferred_element_type=F32)
-    ).astype(BF)
+    pairs = (attn_space, hidden, attn_time, grad_cols, dqkv, cot_cols.reshape(-1, width))
+    head_grads, sums = space_backward(head_blocks, o_rows, lse, grads, pairs)
     block_out = exchange(out_cols.reshape(by_frame), "frame").reshape(hidden_in.shape)
     grad_hidden = exchange(grad_cols.reshape(by_frame), "frame").reshape(hidden_in.shape)
-    back = exchange(space_backward(head_blocks, o_rows, lse, grads), "space")
-    return (block_out, grad_hidden, *join_heads(back), *sums)
+    back = exchange(head_grads, "space")
+    rows_dev = TILE_ROWS // HEADS
+    own = lax.dynamic_slice_in_dim(sums, lax.axis_index("space") * rows_dev, rows_dev, 1)
+    own = own.transpose(1, 0, 2).reshape(rows_dev, -1).astype(F32)
+    cuts = (own[:, :width], own[:, width : 4 * width], own[:, 4 * width : 5 * width])
+    return (block_out, grad_hidden, *join_heads(back), *cuts)
 
 
 def solution(mesh):

time: 446 us -> 365 us (0.82)
  waiting for transfers between devices: 159 us -> 31.1 us
  Pallas kernels: 121 us -> 197 us
  matrix products: 18.7 us -> 0 us
  between operations: 14.1 us -> 0.94 us
  blocking collectives: 106 us -> 101 us
    unnamed x2 -> x0, waiting for transfers between devices: 123 us -> none
    pallas_call x0 -> x1, Pallas kernels: none -> 112 us  [space_backward(): pl.pallas_call(space_backward_body, out_shape=(shape(blocks.shape, BF), s...]
    pallas_call x5 -> x4, Pallas kernels: 121 us -> 85.2 us  [kernel_call(): pl.pallas_call(body, out_shape=out_shape, scratch_shapes=scratch_shapes,...]
    dot_general x4 -> x0, matrix products: 18.7 us -> none  [the longest x3 15.9 us: grad_terms(): lax.dot_general(rows, grads, (((0,), (0,)), ((), ())), preferred_element_...]
    all_to_all x4, waiting for transfers between devices: 36.2 us -> 31.1 us  [exchange(): return lax.all_to_all(blocks, axis, split_axis=0, concat_axis=0, tiled=True)]
    all_to_all x4, blocking collectives: 106 us -> 101 us  [exchange(): return lax.all_to_all(blocks, axis, split_axis=0, concat_axis=0, tiled=True)]
  transfers between devices with their start and end apart: 5 -> 4, of which waited for: 3 -> 2; matrix products, arithmetic and copies ran while one was open for 1% -> 1% of each run, Pallas kernels for 21% -> 43%
where the time goes in v2:
time: 365 us; the launch traced here: 361 us
  Pallas kernels  197 us (54%)
  blocking collectives  101 us (28%)
  waiting for transfers between devices  31.1 us (9%)
  starting transfers between devices  22.7 us (6%)
  local copies, waits for them, and re-layouts  7.55 us (2%)
    pallas_call x1, Pallas kernels, space_backward(): pl.pallas_call(space_backward_body, out_shape=(shape(blocks.shape, BF), s...  112 us
    all_to_all x4, blocking collectives, exchange(): return lax.all_to_all(blocks, axis, split_axis=0, concat_axis=0, tiled=True)  101 us
    pallas_call x4, Pallas kernels, kernel_call(): pl.pallas_call(body, out_shape=out_shape, scratch_shapes=scratch_shapes,...  85.2 us
    all_to_all x4, waiting for transfers between devices, exchange(): return lax.all_to_all(blocks, axis, split_axis=0, concat_axis=0, tiled=True)  31.1 us
    all_to_all x4, starting transfers between devices, exchange(): return lax.all_to_all(blocks, axis, split_axis=0, concat_axis=0, tiled=True)  22.7 us
  transfers between devices with their start and end apart: 4, of which 2 were waited for; matrix products, arithmetic and copies ran while one was open for 1% of the time, Pallas kernels for 43%

profile of v2, /device:TPU:1, one launch (start us, length us, event | category | flops | bytes accessed | tf_op | source)
XLA Modules:
  0.0 360.8 jit_solution(126112290041402285)
XLA Ops:
  0.6 6.9 %all-to-all-start.3 = ((bf16[8,32,1152]{2,1,0:T(8,128)(2,1)}), bf16[8,32,1152]{2,1,0:T(8,128)(2,1)S(1)}, u32[]{:S(2)}, u32[]{:S(2)}) async-start(bf16[8,32,1152]{2,1,0:T(8,128)(2,1)} %bitcast.25), calls=%async_computation.3 | async-start | bytes 1179648 | tf_op jit(solution)/shard_map/all_to_all | solution.py:561
  7.5 3.2 shard_map.143
  10.8 6.6 %all-to-all-done.3.cot_ref = bf16[8,32,1152]{2,1,0:T(8,128)(2,1)S(1)} async-done(((bf16[8,32,1152]{2,1,0:T(8,128)(2,1)}), bf16[8,32,1152]{2,1,0:T(8,128)(2,1)S(1)}, u32[]{:S(2)}, u32[]{:S(2)}) %all-to-all-start.3) | async-done | bytes 589856 | tf_op jit(solution)/shard_map/all_to_all | solution.py:561
  17.4 0.0 copy-start.2
  17.4 35.5 %all_to_all.40.x_ref = bf16[16,3,80,256]{3,2,1,0:T(8,128)(2,1)} all-to-all(bf16[16,3,80,256]{3,2,1,0:T(8,128)(2,1)} %shard_map.143), channel_id=1, replica_groups=mesh['frame'=8,'space'=16] {'space'}, dimensions={0} | all-to-all | bytes 3932160 | tf_op jit(solution)/shard_map/all_to_all | solution.py:561
  52.9 0.0 copy-done.2
  52.9 3.5 all-to-all-start.2
  56.5 40.5 %shard_map.144 = (bf16[8,16,32,128]{3,2,1,0:T(8,128)(2,1)}, f32[16,80,256]{2,1,0:T(8,128)}, f32[16,8,256]{2,1,0:T(8,128)}) custom-call(bf16[16,3,80,256]{3,2,1,0:T(8,128)(2,1)} %all_to_all.40.x_ref), custom_call_target="tpu_custom_call" | custom-call | flops 8589934592 | bytes 5242880 | tf_op jit(solution)/shard_map/pallas_call | solution.py:20
  97.0 0.0 all-to-all-done.2.hidden_in_ref
  97.0 0.0 copy-start.3
  97.0 25.5 %all_to_all.41 = bf16[128,32,128]{2,1,0:T(8,128)(2,1)} all-to-all(bf16[128,32,128]{2,1,0:T(8,128)(2,1)} %bitcast.24), channel_id=1, replica_groups=mesh['frame'=8,'space'=16] {'frame','space'}, dimensions={0} | all-to-all | bytes 2097152 | tf_op jit(solution)/shard_map/all_to_all | solution.py:561
  122.5 0.0 copy-done.3
  122.5 38.4 %shard_map.145 = (bf16[8,16,32,128]{3,2,1,0:T(8,128)(2,1)}, bf16[256,1152]{1,0:T(8,128)(2,1)}, bf16[256,1152]{1,0:T(8,128)(2,1)}, bf16[256,1152]{1,0:T(8,128)(2,...) custom-call(bf16[8,16,32,128]{3,2,1,0:T(8,128)(2,1)} %bitcast.23, ...), custom_call_target="tpu_custom_call" | custom-call | flops 6794772480 | bytes 20971520 | tf_op jit(solution)/shard_map/pallas_call | solution.py:20
  161.0 13.8 %all_to_all.42 = bf16[8,32,1152]{2,1,0:T(8,128)(2,1)} all-to-all(bf16[8,32,1152]{2,1,0:T(8,128)(2,1)} %bitcast.27), channel_id=1, replica_groups=mesh['frame'=8,'space'=16] {'frame'}, dimensions={0} | all-to-all | bytes 1179648 | tf_op jit(solution)/shard_map/all_to_all | solution.py:561
  174.8 25.6 %all_to_all.43 = bf16[128,32,128]{2,1,0:T(8,128)(2,1)} all-to-all(bf16[128,32,128]{2,1,0:T(8,128)(2,1)} %bitcast.22), channel_id=1, replica_groups=mesh['frame'=8,'space'=16] {'frame','space'}, dimensions={0} | all-to-all | bytes 2097152 | tf_op jit(solution)/shard_map/all_to_all | solution.py:561
  200.4 3.5 all-to-all-start.4
  204.0 111.9 %shard_map.146 = (bf16[16,3,80,256]{3,2,1,0:T(8,128)(2,1)}, bf16[16,144,384]{2,1,0:T(8,128)(2,1)}) custom-call(bf16[16,3,80,256]{3,2,1,0:T(8,128)(2,1)} %all_to_all.40.x_ref, f32[16,80,256]{2,1,0:T(8,128)} %get-tuple-element.26.o_rows_ref, f32[16,8,256]{2,1,0:T(8,128)} %get-tuple-element.27.lse_ref, bf16[8,16,32,128]{3,2,1,0:T(8,128)(2,1)} %bitcast.21, ...), custom_call_target="tpu_custom_call" | custom-call | flops 21474836480 | bytes 16777216 | tf_op jit(solution)/shard_map/pallas_call | solution.py:439
  315.8 0.0 all-to-all-done.4
  315.8 0.0 copy-start.1
  315.8 0.8 copy-done.1
  316.7 8.8 %all-to-all-start.7 = ((bf16[16,3,80,256]{3,2,1,0:T(8,128)(2,1)}), bf16[16,3,80,256]{3,2,1,0:T(8,128)(2,1)S(1)}, u32[]{:S(2)}, u32[]{:S(2)}) async-start(bf16[16,3,80,256]{3,2,1,0:T(8,128)(2,1)} %get-tuple-element.33), calls=%async_computation.7 | async-start | bytes 3932160 | tf_op jit(solution)/shard_map/all_to_all | solution.py:561
  325.4 1.0 convert_bitcast_fusion
  326.4 0.1 copy.16
  326.5 0.1 copy.17
  326.7 0.7 slice.13
  327.4 0.7 fusion
  328.0 24.4 %all-to-all-done.7.in_ref = bf16[16,3,80,256]{3,2,1,0:T(8,128)(2,1)S(1)} async-done(((bf16[16,3,80,256]{3,2,1,0:T(8,128)(2,1)}), bf16[16,3,80,256]{3,2,1,0:T(8,128)(2,1)S(1)}, u32[]{:S(2)}, u32[]{:S(2)}) %all-to-all-start.7) | async-done | bytes 1966112 | tf_op jit(solution)/shard_map/all_to_all | solution.py:561
  352.4 0.0 copy-start
  352.4 1.3 copy-done
  353.8 3.0 shard_map.147
  356.7 1.9 copy.20
  358.7 1.9 copy.21
  (1 shorter events, 0.0 us)
Async XLA Ops:
  0.6 16.8 %all-to-all-start.3 = ((bf16[8,32,1152]{2,1,0:T(8,128)(2,1)}), bf16[8,32,1152]{2,1,0:T(8,128)(2,1)S(1)}, u32[]{:S(2)}, u32[]{:S(2)}) async-start(bf16[8,32,1152]{2,1,0:T(8,128)(2,1)} %bitcast.25), calls=%async_computation.3 | async-start | bytes 1179648 | tf_op jit(solution)/shard_map/all_to_all | solution.py:561
  17.4 35.6 %copy-start.2 = (bf16[8,32,1152]{2,1,0:T(8,128)(2,1)}, bf16[8,32,1152]{2,1,0:T(8,128)(2,1)S(1)}, u32[]{:S(2)}) copy-start(bf16[8,32,1152]{2,1,0:T(8,128)(2,1)S(1)} %all-to-all-done.3.cot_ref) | copy-start | bytes 1769476
  52.9 44.0 %all-to-all-start.2 = ((bf16[8,32,1152]{2,1,0:T(8,128)(2,1)}), bf16[8,32,1152]{2,1,0:T(8,128)(2,1)S(1)}, u32[]{:S(2)}, u32[]{:S(2)}) async-start(bf16[8,32,1152]{2,1,0:T(8,128)(2,1)} %bitcast.2), calls=%async_computation.2 | async-start | bytes 1179648 | tf_op jit(solution)/shard_map/all_to_all | solution.py:561
  97.0 25.5 %copy-start.3 = (bf16[8,32,1152]{2,1,0:T(8,128)(2,1)}, bf16[8,32,1152]{2,1,0:T(8,128)(2,1)S(1)}, u32[]{:S(2)}) copy-start(bf16[8,32,1152]{2,1,0:T(8,128)(2,1)S(1)} %all-to-all-done.2.hidden_in_ref) | copy-start | bytes 1769476
  200.4 115.4 %all-to-all-start.4 = ((bf16[8,32,1152]{2,1,0:T(8,128)(2,1)}), bf16[8,32,1152]{2,1,0:T(8,128)(2,1)S(1)}, u32[]{:S(2)}, u32[]{:S(2)}) async-start(bf16[8,32,1152]{2,1,0:T(8,128)(2,1)} %bitcast.4), calls=%async_computation.4 | async-start | bytes 1179648 | tf_op jit(solution)/shard_map/all_to_all | solution.py:561
  315.8 0.8 copy-start.1
  316.7 35.8 %all-to-all-start.7 = ((bf16[16,3,80,256]{3,2,1,0:T(8,128)(2,1)}), bf16[16,3,80,256]{3,2,1,0:T(8,128)(2,1)S(1)}, u32[]{:S(2)}, u32[]{:S(2)}) async-start(bf16[16,3,80,256]{3,2,1,0:T(8,128)(2,1)} %get-tuple-element.33), calls=%async_computation.7 | async-start | bytes 3932160 | tf_op jit(solution)/shard_map/all_to_all | solution.py:561
  352.4 1.3 copy-start

commit v3 on v2

--- a/solution.py
+++ b/solution.py
@@ -61,28 +61,14 @@
     return jnp.where(at < 3, -1.0, 0.0).astype(BF)
 
 
-def split_heads_body(q_ref, k_ref, v_ref, out_ref):
-    tokens = q_ref.shape[1]
+def split_heads(ref, out_ref, i):
+    tokens = ref.shape[1]
     at = lax.broadcasted_iota(jnp.int32, (ROWS - HD, tokens), 0)
-    ones_row = jnp.where(at == 0, 1.0, 0.0)
-    for i, ref in enumerate((q_ref, k_ref, v_ref)):
-        flipped = ref[0].astype(F32).T
-        for h in range(HEADS):
-            fill = ones_row if i == 2 else jnp.zeros_like(ones_row)
-            block = jnp.concatenate([flipped[h * HD : (h + 1) * HD], fill], axis=0)
-            out_ref[h, i] = block.astype(BF)
-
-
-def split_heads(query, key_rows, value_rows):
-    tokens, width = query.shape[1:]
-    return kernel_call(
-        split_heads_body,
-        shape((HEADS, 3, ROWS, tokens), BF),
-        [],
-        0,
-        3 * tokens * width * 5,
-        (query, key_rows, value_rows),
-    )
+    fill = jnp.where(at == 0, 1.0 if i == 2 else 0.0, 0.0)
+    flipped = ref[0].astype(F32).T
+    for h in range(HEADS):
+        block = jnp.concatenate([flipped[h * HD : (h + 1) * HD], fill], axis=0)
+        out_ref[h, i] = block.astype(BF)
 
 
 def join_heads_body(in_ref, q_ref, k_ref, v_ref):
@@ -99,12 +85,93 @@
     )
 
 
+def copy_to(src, dst, send_sem, recv_sem, device):
+    return pltpu.make_async_remote_copy(
+        src_ref=src,
+        dst_ref=dst,
+        send_sem=send_sem,
+        recv_sem=recv_sem,
+        device_id=device,
+        device_id_type=pl.DeviceIdType.MESH,
+    )
+
+
+def signal_all(barrier, peers):
+    for peer in peers:
+        pl.semaphore_signal(barrier, inc=1, device_id=peer, device_id_type=pl.DeviceIdType.MESH)
+
+
+def rows_of(ref, i, count):
+    return ref.at[pl.ds(pl.multiple_of(i * count, count), count)]
+
+
 def scaled_query(block):
     return two_parts(block.astype(F32) * (SCALE * LOG2E))
 
 
-def space_forward_body(x_ref, o_ref, o_rows_ref, lse_ref, k_nat, v_rows):
+def space_forward_body(
+    q_ref,
+    k_ref,
+    v_ref,
+    hidden_ref,
+    cot_ref,
+    x_ref,
+    hidden_cols_ref,
+    cot_cols_ref,
+    o_ref,
+    o_rows_ref,
+    lse_ref,
+    packed,
+    k_nat,
+    v_rows,
+    s_one,
+    s_two,
+    send_x,
+    recv_x,
+    send_f,
+    recv_f,
+):
     blocks, _, _, width = x_ref.shape
+    frames, positions, _ = hidden_cols_ref.shape
+    seq = blocks * width
+    frame, space = lax.axis_index("frame"), lax.axis_index("space")
+    others = [lax.rem(space + i, blocks) for i in range(1, blocks)]
+    other_frames = [lax.rem(frame + i, frames) for i in range(1, frames)]
+    peers = [(frame, to) for to in others] + [(to, space) for to in other_frames]
+    barrier = pltpu.get_barrier_semaphore()
+    signal_all(barrier, peers)
+
+    waits = []
+    for i, ref in ((1, k_ref), (2, v_ref), (0, q_ref)):
+        split_heads(ref, packed, i)
+        if not waits:
+            pl.semaphore_wait(barrier, len(peers))
+        for n, to in enumerate(others):
+            c = copy_to(
+                packed.at[to, i],
+                x_ref.at[space, i],
+                send_x.at[i, n],
+                recv_x.at[i, n],
+                (frame, to),
+            )
+            c.start()
+            waits.append(c)
+        x_ref[space, i] = packed[space, i]
+    moves = []
+    for i, (ref, out) in enumerate(((hidden_ref, hidden_cols_ref), (cot_ref, cot_cols_ref))):
+        for n, to in enumerate(other_frames):
+            c = copy_to(
+                rows_of(ref.at[0], to, positions),
+                out.at[frame],
+                send_f.at[i, n],
+                recv_f.at[i, n],
+                (to, space),
+            )
+            c.start()
+            moves.append(c)
+        out[frame] = rows_of(ref.at[0], frame, positions)[...]
+    for c in waits[: 2 * len(others)]:
+        c.wait()
 
     def prepare(j, _):
         at = pl.ds(pl.multiple_of(j * width, width), width)
@@ -115,38 +182,88 @@
 
     lax.fori_loop(0, blocks, prepare, 0)
 
-    def step(j, _):
+    for c in waits[2 * len(others) :]:
+        c.wait()
+
+    def score(j, s_ref):
         q_block = jnp.concatenate(scaled_query(x_ref[j, 0]), axis=0)
-        scores = dot(k_nat[...], q_block)
-        top = jnp.max(scores, axis=0, keepdims=True)
-        probs = jnp.exp2(scores - top).astype(BF)
-        mixed = dot(v_rows[...], probs)
+        top = None
+        for c in range(CHUNKS):
+            at = slice(c * seq // CHUNKS, (c + 1) * seq // CHUNKS)
+            s = dot(k_nat[at, :], q_block)
+            s_ref[at, :] = s
+            best = jnp.max(s, axis=0, keepdims=True)
+            top = best if top is None else jnp.maximum(top, best)
+        return top
+
+    def both(j, s_ref, top, after, s_after):
+        q_block = jnp.concatenate(scaled_query(x_ref[after, 0]), axis=0)
+        top_after = None
+        mixed = jnp.zeros((ROWS, width), F32)
+        for c in range(CHUNKS):
+            at = slice(c * seq // CHUNKS, (c + 1) * seq // CHUNKS)
+            s = dot(k_nat[at, :], q_block)
+            s_after[at, :] = s
+            best = jnp.max(s, axis=0, keepdims=True)
+            top_after = best if top_after is None else jnp.maximum(top_after, best)
+            probs = jnp.exp2(s_ref[at, :] - top).astype(BF)
+            mixed = mixed + dot(v_rows[:, at], probs)
         total = mixed[HD : HD + 1]
         mixed = mixed / total
         o_rows_ref[j] = mixed
         lse_ref[j] = jnp.broadcast_to(top + jnp.log2(total), (8, width))
         filled = jnp.concatenate([mixed[:HD], jnp.zeros((128 - HD, width), F32)], axis=0)
         o_ref[:, j] = filled.T.astype(BF).reshape(o_ref.shape[0], o_ref.shape[2], 128)
-        return 0
-
-    lax.fori_loop(0, blocks, step, 0)
-
-
-def space_forward(blocks, frames):
-    count, _, _, width = blocks.shape
-    seq = count * width
-    return kernel_call(
+        return top_after
+
+    def two_steps(i, top):
+        j = 2 * i
+        top = both(j, s_one, top, j + 1, s_two)
+        return both(j + 1, s_two, top, jnp.minimum(j + 2, blocks - 1), s_one)
+
+    lax.fori_loop(0, blocks // 2, two_steps, score(0, s_one))
+    for c in moves:
+        c.wait()
+
+
+CHUNKS = 8
+
+
+def space_forward(query, key_rows, value_rows, hidden_in, cot, frames):
+    tokens, model = query.shape[1:]
+    seq = HEADS * tokens
+    dma = pltpu.SemaphoreType.DMA
+    cols = shape((frames, tokens // frames, model), BF)
+    return pl.pallas_call(
         space_forward_body,
-        (
-            shape((frames, count, width // frames, 128), BF),
-            shape((count, ROWS, width), F32),
-            shape((count, 8, width), F32),
+        out_shape=(
+            shape((HEADS, 3, ROWS, tokens), BF),
+            cols,
+            cols,
+            shape((frames, HEADS, tokens // frames, 128), BF),
+            shape((HEADS, ROWS, tokens), F32),
+            shape((HEADS, 8, tokens), F32),
         ),
-        [pltpu.VMEM((seq, 2 * ROWS), BF), pltpu.VMEM((ROWS, seq), BF)],
-        4 * seq * seq * 128,
-        5 * 2**20,
-        (blocks,),
-    )
+        in_specs=[pl.BlockSpec(memory_space=pltpu.VMEM)] * 5,
+        out_specs=[pl.BlockSpec(memory_space=pltpu.VMEM)] * 6,
+        scratch_shapes=[
+            pltpu.VMEM((HEADS, 3, ROWS, tokens), BF),
+            pltpu.VMEM((seq, 2 * ROWS), BF),
+            pltpu.VMEM((ROWS, seq), BF),
+            pltpu.VMEM((seq, tokens), F32),
+            pltpu.VMEM((seq, tokens), F32),
+            dma((3, HEADS - 1)),
+            dma((3, HEADS - 1)),
+            dma((2, frames - 1)),
+            dma((2, frames - 1)),
+        ],
+        compiler_params=pltpu.CompilerParams(
+            vmem_limit_bytes=VMEM_BYTES, collective_id=1, has_side_effects=True
+        ),
+        cost_estimate=pl.CostEstimate(
+            flops=4 * seq * seq * 128, bytes_accessed=8 * 2**20, transcendentals=0
+        ),
+    )(query, key_rows, value_rows, hidden_in, cot)
 
 
 Q_STEP = 1024
@@ -175,12 +292,13 @@
 
 
 def backward_steps(
-    first, last, x_ref, out_ref, q_aug, g_aug, q_rows, g_rows, p_buf, ds_buf, dq_sum
+    first, last, done, x_ref, out_ref, q_aug, g_aug, q_rows, g_rows, p_buf, ds_buf, dq_sum
 ):
     blocks, _, _, width = x_ref.shape
     seq = blocks * width
 
-    def step(j, _):
+    def step(t, _):
+        j = lax.rem(lax.axis_index("space") + 1 + t, blocks)
         k_block = x_ref[j, 1]
         v_block = x_ref[j, 2]
         k_aug = jnp.concatenate([k_block, k_block, minus_rows(16, width)], axis=0)
@@ -197,20 +315,10 @@
 
         out_ref[j, 1] = (dot(q_rows[...], ds_buf[...]) * SCALE).astype(BF)
         out_ref[j, 2] = dot(g_rows[...], p_buf[...]).astype(BF)
+        done(t, last)
         return 0
 
     lax.fori_loop(first, last, step, 0)
-
-
-def backward_finish(out_ref, dq_sum):
-    blocks, _, _, width = out_ref.shape
-
-    def finish(j, _):
-        at = pl.ds(pl.multiple_of(j * width, width), width)
-        out_ref[j, 0] = (dq_sum[at, :] * SCALE).T.astype(BF)
-        return 0
-
-    lax.fori_loop(0, blocks, finish, 0)
 
 
 def add_into(target, terms, lead):
@@ -243,8 +351,12 @@
     gh_ref,
     dqkv_ref,
     cot_ref,
+    out_cols_ref,
+    back_ref,
+    sums_ref,
+    grad_hidden_ref,
+    block_out_ref,
     out_ref,
-    sums_ref,
     q_aug,
     g_aug,
     q_rows,
@@ -261,7 +373,6 @@
     lo_in,
     hi_in,
     mine,
-    gathered,
     send1,
     recv1,
     send2,
@@ -272,6 +383,12 @@
     recv4,
     send6,
     recv6,
+    send_f,
+    recv_f,
+    send_kv,
+    recv_kv,
+    send_q,
+    recv_q,
 ):
     frame, space = lax.axis_index("frame"), lax.axis_index("space")
     z, lo = lax.div(frame, 2), lax.rem(frame, 2)
@@ -290,20 +407,12 @@
     hi_peer = (frame, x * 4 + (1 - hi) * 2 + core)
     core_peer = (frame, x * 4 + hi * 2 + 1 - core)
 
-    def copy(src, dst, send_sem, recv_sem, device):
-        return pltpu.make_async_remote_copy(
-            src_ref=src,
-            dst_ref=dst,
-            send_sem=send_sem,
-            recv_sem=recv_sem,
-            device_id=device,
-            device_id_type=pl.DeviceIdType.MESH,
-        )
-
+    copy = copy_to
+    others = [lax.rem(space + i, 16) for i in range(1, 16)]
+    other_frames = [lax.rem(frame + i, 8) for i in range(1, 8)]
+    peers = [(frame, to) for to in others] + [(to, space) for to in other_frames]
     barrier = pltpu.get_barrier_semaphore()
-    peers = [space_peer(i) for i in range(1, 16)] + [z_peer(i) for i in range(1, 4)] + [lo_peer]
-    for peer in peers:
-        pl.semaphore_signal(barrier, inc=1, device_id=peer, device_id_type=pl.DeviceIdType.MESH)
+    signal_all(barrier, peers)
 
     for t, (rows_ref, grads_ref, offset) in enumerate(
         [(attn_space_ref, gh_ref, c) for c in range(3)]
@@ -333,12 +442,46 @@
     ]
     for c in first:
         c.start()
+    moves = []
+    for i, (ref, out) in enumerate(((gh_ref, grad_hidden_ref), (out_cols_ref, block_out_ref))):
+        positions = out.shape[1]
+        for n, to in enumerate(other_frames):
+            c = copy(
+                rows_of(ref, to, positions),
+                out.at[frame],
+                send_f.at[i, n],
+                recv_f.at[i, n],
+                (to, space),
+            )
+            c.start()
+            moves.append(c)
+        out[frame] = rows_of(ref, frame, positions)[...]
 
     state = (q_aug, g_aug, q_rows, g_rows)
     backward_prepare(x_ref, o_rows_ref, lse_ref, g_ref, *state, dq_sum)
 
     def attend(start, stop):
-        backward_steps(start, stop, x_ref, out_ref, *state, p_buf, ds_buf, dq_sum)
+        backward_steps(start, stop, send_step, x_ref, out_ref, *state, p_buf, ds_buf, dq_sum)
+
+    def key_grads(t):
+        to = lax.rem(space + 1 + t, 16)
+        return copy(
+            out_ref.at[to, pl.ds(1, 2)],
+            back_ref.at[space, pl.ds(1, 2)],
+            send_kv.at[t],
+            recv_kv.at[t],
+            (frame, to),
+        )
+
+    def query_grads(t):
+        to = lax.rem(space + 1 + t, 16)
+        return copy(
+            out_ref.at[to, 0], back_ref.at[space, 0], send_q.at[t], recv_q.at[t], (frame, to)
+        )
+
+    def send_step(t, stop):
+        if stop < 16:
+            key_grads(t).start()
 
     attend(0, STAGES[0])
 
@@ -409,23 +552,39 @@
     fifth = copy(half.at[lo, z, x, 1 - hi], hi_in, send4.at[1], recv4.at[1], hi_peer)
     fifth.start()
 
-    attend(STAGES[3], 16)
+    attend(STAGES[3], 15)
+    attend(15, 16)
 
     fifth.wait()
     total = (half[lo, z, x, hi].astype(F32) + hi_in[...].astype(F32)).astype(BF)
     mine[...] = total
     sixth = [
-        copy(mine, gathered.at[i - 1], send6.at[i - 1], recv6.at[i - 1], space_peer(i))
+        copy(mine, sums_ref.at[space], send6.at[i - 1], recv6.at[i - 1], space_peer(i))
         for i in range(1, 16)
     ]
     for c in sixth:
         c.start()
-
-    backward_finish(out_ref, dq_sum)
     sums_ref[space] = total
-    for i, c in enumerate(sixth):
+
+    def finish(t, _):
+        to = lax.rem(space + 1 + t, 16)
+        at = pl.ds(pl.multiple_of(to * width, width), width)
+        out_ref[to, 0] = (dq_sum[at, :] * SCALE).T.astype(BF)
+
+        @pl.when(t < 15)
+        def _():
+            query_grads(t).start()
+
+        return 0
+
+    width = x_ref.shape[3]
+    lax.fori_loop(0, 16, finish, 0)
+    back_ref[space] = out_ref[space]
+    for c in moves + sixth:
         c.wait()
-        sums_ref[lax.rem(space + 15 - i, 16)] = gathered[i]
+    for t in range(15):
+        key_grads(t).wait()
+        query_grads(t).wait()
 
 
 STAGES = (3, 10, 13, 15)
@@ -435,13 +594,15 @@
     count, _, _, width = blocks.shape
     seq = count * width
     tile = (TILE_ROWS, TILE_COLS)
+    by_frame = shape((8, width // 8, HEADS * HD), BF)
     dma = pltpu.SemaphoreType.DMA
     return pl.pallas_call(
         space_backward_body,
-        out_shape=(shape(blocks.shape, BF), shape((16,) + tile, BF)),
-        in_specs=[pl.BlockSpec(memory_space=pltpu.VMEM)] * 10,
-        out_specs=[pl.BlockSpec(memory_space=pltpu.VMEM)] * 2,
+        out_shape=(shape(blocks.shape, BF), shape((16,) + tile, BF), by_frame, by_frame),
+        in_specs=[pl.BlockSpec(memory_space=pltpu.VMEM)] * 11,
+        out_specs=[pl.BlockSpec(memory_space=pltpu.VMEM)] * 4,
         scratch_shapes=[
+            pltpu.VMEM(blocks.shape, BF),
             pltpu.VMEM((seq, 2 * ROWS + 16), BF),
             pltpu.VMEM((seq, ROWS + 16), BF),
             pltpu.VMEM((ROWS, seq), BF),
@@ -458,7 +619,6 @@
             pltpu.VMEM((2,) + tile, BF),
             pltpu.VMEM(tile, BF),
             pltpu.VMEM(tile, BF),
-            pltpu.VMEM((15,) + tile, BF),
             dma((2, 4)),
             dma((2, 4)),
             dma((2, 3)),
@@ -467,6 +627,12 @@
             dma((2, 3)),
             dma((2,)),
             dma((2,)),
+            dma((15,)),
+            dma((15,)),
+            dma((2, 7)),
+            dma((2, 7)),
+            dma((15,)),
+            dma((15,)),
             dma((15,)),
             dma((15,)),
         ],
@@ -569,25 +735,20 @@
 def shards(
     hidden_in, query_space, key_space, value_space, cotangent, w_space_out, w_time_qkv, w_time_out
 ):
-    tile_rows, width = hidden_in.shape[1:]
+    width = hidden_in.shape[2]
     frames = lax.axis_size("frame")
-    positions = tile_rows // frames
-    by_frame = (frames, positions, width)
-
-    head_blocks = exchange(split_heads(query_space, key_space, value_space), "space")
-    hidden_cols = exchange(hidden_in.reshape(by_frame), "frame")
-    cot_cols = exchange(cotangent.reshape(by_frame), "frame")
-    mixed, o_rows, lse = space_forward(head_blocks, frames)
+    head_blocks, hidden_cols, cot_cols, mixed, o_rows, lse = space_forward(
+        query_space, key_space, value_space, hidden_in, cotangent, frames
+    )
     attn = exchange_all(mixed)
     g_out, grad_cols, out_cols, attn_space, hidden, attn_time, dqkv = middle(
         attn, hidden_cols, cot_cols, w_space_out, w_time_qkv, w_time_out
     )
     grads = exchange_all(g_out)
-    pairs = (attn_space, hidden, attn_time, grad_cols, dqkv, cot_cols.reshape(-1, width))
-    head_grads, sums = space_backward(head_blocks, o_rows, lse, grads, pairs)
-    block_out = exchange(out_cols.reshape(by_frame), "frame").reshape(hidden_in.shape)
-    grad_hidden = exchange(grad_cols.reshape(by_frame), "frame").reshape(hidden_in.shape)
-    back = exchange(head_grads, "space")
+    pairs = (attn_space, hidden, attn_time, grad_cols, dqkv, cot_cols.reshape(-1, width), out_cols)
+    back, sums, grad_hidden, block_out = space_backward(head_blocks, o_rows, lse, grads, pairs)
+    block_out = block_out.reshape(hidden_in.shape)
+    grad_hidden = grad_hidden.reshape(hidden_in.shape)
     rows_dev = TILE_ROWS // HEADS
     own = lax.dynamic_slice_in_dim(sums, lax.axis_index("space") * rows_dev, rows_dev, 1)
     own = own.transpose(1, 0, 2).reshape(rows_dev, -1).astype(F32)

time: 365 us -> 293 us (0.80)
  blocking collectives: 101 us -> 27.2 us
  Pallas kernels: 197 us -> 232 us
  starting transfers between devices: 22.7 us -> 4.61 us
  waiting for transfers between devices: 31.1 us -> 19.1 us
    all_to_all x4 -> x1, blocking collectives: 101 us -> 27.2 us  [exchange(): return lax.all_to_all(blocks, axis, split_axis=0, concat_axis=0, tiled=True)]
    pallas_call x0 -> x1, Pallas kernels: none -> 58.3 us  [space_forward(): pl.pallas_call(space_forward_body, out_shape=(shape((HEADS, 3, ROWS, toke...]
    pallas_call x4 -> x2, Pallas kernels: 85.2 us -> 41.4 us  [kernel_call(): pl.pallas_call(body, out_shape=out_shape, scratch_shapes=scratch_shapes,...]
    pallas_call x1, Pallas kernels: 112 us -> 132 us  [space_backward(): pl.pallas_call(space_backward_body, out_shape=(shape(blocks.shape, BF), s...]
    all_to_all x4 -> x1, starting transfers between devices: 22.7 us -> 4.61 us  [exchange(): return lax.all_to_all(blocks, axis, split_axis=0, concat_axis=0, tiled=True)]
    all_to_all x4 -> x1, waiting for transfers between devices: 31.1 us -> 19.1 us  [exchange(): return lax.all_to_all(blocks, axis, split_axis=0, concat_axis=0, tiled=True)]
  transfers between devices with their start and end apart: 4 -> 1, of which waited for: 2 -> 1; matrix products, arithmetic and copies ran while one was open for 1% -> 0% of each run, Pallas kernels for 43% -> 0%
where the time goes in v3:
time: 293 us; the launch traced here: 289 us
  Pallas kernels  232 us (79%)
  blocking collectives  27.2 us (9%)
  waiting for transfers between devices  19.1 us (7%)
  starting transfers between devices  4.61 us (2%)
  local copies, waits for them, and re-layouts  4.25 us (1%)
    pallas_call x1, Pallas kernels, space_backward(): pl.pallas_call(space_backward_body, out_shape=(shape(blocks.shape, BF), s...  132 us
    pallas_call x1, Pallas kernels, space_forward(): pl.pallas_call(space_forward_body, out_shape=(shape((HEADS, 3, ROWS, toke...  58.3 us
    pallas_call x2, Pallas kernels, kernel_call(): pl.pallas_call(body, out_shape=out_shape, scratch_shapes=scratch_shapes,...  41.4 us
    all_to_all x1, blocking collectives, exchange(): return lax.all_to_all(blocks, axis, split_axis=0, concat_axis=0, tiled=True)  27.2 us
    all_to_all x1, waiting for transfers between devices, exchange(): return lax.all_to_all(blocks, axis, split_axis=0, concat_axis=0, tiled=True)  19.1 us
  transfers between devices with their start and end apart: 1, of which 1 were waited for; matrix products, arithmetic and copies ran while one was open for 0% of the time, Pallas kernels for 0%

profile of v3, /device:TPU:1, one launch (start us, length us, event | category | flops | bytes accessed | tf_op | source)
XLA Modules:
  0.0 288.7 jit_solution(362781808667694775)
XLA Ops:
  0.6 58.3 %shard_map.143 = (bf16[16,3,80,256]{3,2,1,0:T(8,128)(2,1)}, bf16[8,32,1152]{2,1,0:T(8,128)(2,1)}, bf16[8,32,1152]{2,1,0:T(8,128)(2,1)}, bf16[8,16,32,128]{3,2,1,...) custom-call(bf16[1,256,1152]{2,1,0:T(8,128)(2,1)} %q_ref.1, bf16[1,256,1152]{2,1,0:T(8,128)(2,1)} %k_ref.1, ...), custom_call_target="tpu_custom_call" | custom-call | flops 8589934592 | bytes 8388608 | tf_op jit(solution)/shard_map/pallas_call | solution.py:237
  58.9 27.2 %all_to_all.10 = bf16[128,32,128]{2,1,0:T(8,128)(2,1)} all-to-all(bf16[128,32,128]{2,1,0:T(8,128)(2,1)} %bitcast.18), channel_id=1, replica_groups=mesh['frame'=8,'space'=16] {'frame','space'}, dimensions={0} | all-to-all | bytes 2097152 | tf_op jit(solution)/shard_map/all_to_all | solution.py:727
  86.1 38.4 %shard_map.144 = (bf16[8,16,32,128]{3,2,1,0:T(8,128)(2,1)}, bf16[256,1152]{1,0:T(8,128)(2,1)}, bf16[256,1152]{1,0:T(8,128)(2,1)}, bf16[256,1152]{1,0:T(8,128)(2,...) custom-call(bf16[8,16,32,128]{3,2,1,0:T(8,128)(2,1)} %bitcast.17, ...), custom_call_target="tpu_custom_call" | custom-call | flops 6794772480 | bytes 20971520 | tf_op jit(solution)/shard_map/pallas_call | solution.py:20
  124.5 4.6 %all-to-all-start.1 = ((bf16[128,32,128]{2,1,0:T(8,128)(2,1)}), bf16[128,32,128]{2,1,0:T(8,128)(2,1)S(1)}, u32[]{:S(2)}, u32[]{:S(2)}) async-start(bf16[128,32,128]{2,1,0:T(8,128)(2,1)} %bitcast.16), calls=%async_computation.1 | async-start | bytes 2097152 | tf_op jit(solution)/shard_map/all_to_all | solution.py:727
  129.1 19.1 %all-to-all-done.1 = bf16[128,32,128]{2,1,0:T(8,128)(2,1)S(1)} async-done(((bf16[128,32,128]{2,1,0:T(8,128)(2,1)}), bf16[128,32,128]{2,1,0:T(8,128)(2,1)S(1)}, u32[]{:S(2)}, u32[]{:S(2)}) %all-to-all-start.1) | async-done | bytes 1048608 | tf_op jit(solution)/shard_map/all_to_all | solution.py:727
  148.2 0.0 copy-start
  148.2 1.0 copy-done
  149.2 132.0 %shard_map.145 = (bf16[16,3,80,256]{3,2,1,0:T(8,128)(2,1)}, bf16[16,144,384]{2,1,0:T(8,128)(2,1)}, bf16[8,32,1152]{2,1,0:T(8,128)(2,1)}, bf16[8,32,1152]{2,1,0:T(8,128)(2,1)}) custom-call(bf16[16,3,80,256]{3,2,1,0:T(8,128)(2,1)} %get-tuple-element.28.x_ref, f32[16,80,256]{2,1,0:T(8,128)} %get-tuple-element.29.o_rows_ref, ...), custom_call_target="tpu_custom_call" | custom-call | flops 21474836480 | bytes 16777216 | tf_op jit(solution)/shard_map/pallas_call | solution.py:599
  281.2 1.0 convert_bitcast_fusion
  282.2 0.1 copy.16
  282.3 0.0 copy-start.2
  282.4 0.1 copy.17
  282.5 0.0 copy-start.1
  282.5 0.7 slice.13
  283.2 0.7 fusion
  283.9 3.0 %shard_map.146 = (bf16[1,256,1152]{2,1,0:T(8,128)(2,1)}, bf16[1,256,1152]{2,1,0:T(8,128)(2,1)}, bf16[1,256,1152]{2,1,0:T(8,128)(2,1)}) custom-call(bf16[16,3,80,256]{3,2,1,0:T(8,128)(2,1)} %get-tuple-element.43.in_ref), custom_call_target="tpu_custom_call" | custom-call | bytes 4423680 | tf_op jit(solution)/shard_map/pallas_call | solution.py:20
  286.9 0.0 copy-done.2
  286.9 0.8 copy.20
  287.7 0.0 copy-done.1
  287.7 0.8 copy.21
  (1 shorter events, 0.0 us)
Async XLA Ops:
  124.5 23.7 %all-to-all-start.1 = ((bf16[128,32,128]{2,1,0:T(8,128)(2,1)}), bf16[128,32,128]{2,1,0:T(8,128)(2,1)S(1)}, u32[]{:S(2)}, u32[]{:S(2)}) async-start(bf16[128,32,128]{2,1,0:T(8,128)(2,1)} %bitcast.16), calls=%async_computation.1 | async-start | bytes 2097152 | tf_op jit(solution)/shard_map/all_to_all | solution.py:727
  148.2 1.0 copy-start
  282.3 4.5 %copy-start.2 = (bf16[8,32,1152]{2,1,0:T(8,128)(2,1)S(1)}, bf16[8,32,1152]{2,1,0:T(8,128)(2,1)}, u32[]{:S(2)}) copy-start(bf16[8,32,1152]{2,1,0:T(8,128)(2,1)} %get-tuple-element.41) | copy-start | bytes 1769476
  282.5 5.2 %copy-start.1 = (bf16[8,32,1152]{2,1,0:T(8,128)(2,1)S(1)}, bf16[8,32,1152]{2,1,0:T(8,128)(2,1)}, u32[]{:S(2)}) copy-start(bf16[8,32,1152]{2,1,0:T(8,128)(2,1)} %get-tuple-element.42) | copy-start | bytes 1769476

commit v4 on v3

--- a/solution.py
+++ b/solution.py
@@ -118,10 +118,12 @@
     x_ref,
     hidden_cols_ref,
     cot_cols_ref,
-    o_ref,
+    attn_ref,
     o_rows_ref,
     lse_ref,
     packed,
+    o_buf,
+    heads_in,
     k_nat,
     v_rows,
     s_one,
@@ -130,6 +132,10 @@
     recv_x,
     send_f,
     recv_f,
+    send_o,
+    recv_o,
+    send_a,
+    recv_a,
 ):
     blocks, _, _, width = x_ref.shape
     frames, positions, _ = hidden_cols_ref.shape
@@ -196,7 +202,17 @@
             top = best if top is None else jnp.maximum(top, best)
         return top
 
-    def both(j, s_ref, top, after, s_after):
+    def block_at(t):
+        return lax.rem(space + 1 + t, blocks)
+
+    def send_block(t):
+        to = block_at(t)
+        return copy_to(
+            o_buf.at[to], heads_in.at[space], send_o.at[t], recv_o.at[t], (frame, to)
+        )
+
+    def both(t, s_ref, top, t_after, s_after):
+        j, after = block_at(t), block_at(t_after)
         q_block = jnp.concatenate(scaled_query(x_ref[after, 0]), axis=0)
         top_after = None
         mixed = jnp.zeros((ROWS, width), F32)
@@ -213,7 +229,12 @@
         o_rows_ref[j] = mixed
         lse_ref[j] = jnp.broadcast_to(top + jnp.log2(total), (8, width))
         filled = jnp.concatenate([mixed[:HD], jnp.zeros((128 - HD, width), F32)], axis=0)
-        o_ref[:, j] = filled.T.astype(BF).reshape(o_ref.shape[0], o_ref.shape[2], 128)
+        o_buf[j] = filled.T.astype(BF).reshape(frames, positions, 128)
+
+        @pl.when(t < blocks - 1)
+        def _():
+            send_block(t).start()
+
         return top_after
 
     def two_steps(i, top):
@@ -221,7 +242,17 @@
         top = both(j, s_one, top, j + 1, s_two)
         return both(j + 1, s_two, top, jnp.minimum(j + 2, blocks - 1), s_one)
 
-    lax.fori_loop(0, blocks // 2, two_steps, score(0, s_one))
+    lax.fori_loop(0, blocks // 2, two_steps, score(block_at(0), s_one))
+    heads_in[space] = o_buf[space]
+    for t in range(blocks - 1):
+        send_block(t).wait()
+    for n, to in enumerate(other_frames):
+        c = copy_to(
+            heads_in.at[:, to], attn_ref.at[frame], send_a.at[n], recv_a.at[n], (to, space)
+        )
+        c.start()
+        moves.append(c)
+    attn_ref[frame] = heads_in[:, frame]
     for c in moves:
         c.wait()
 
@@ -248,6 +279,8 @@
         out_specs=[pl.BlockSpec(memory_space=pltpu.VMEM)] * 6,
         scratch_shapes=[
             pltpu.VMEM((HEADS, 3, ROWS, tokens), BF),
+            pltpu.VMEM((HEADS, frames, tokens // frames, 128), BF),
+            pltpu.VMEM((HEADS, frames, tokens // frames, 128), BF),
             pltpu.VMEM((seq, 2 * ROWS), BF),
             pltpu.VMEM((ROWS, seq), BF),
             pltpu.VMEM((seq, tokens), F32),
@@ -256,6 +289,10 @@
             dma((3, HEADS - 1)),
             dma((2, frames - 1)),
             dma((2, frames - 1)),
+            dma((HEADS - 1,)),
+            dma((HEADS - 1,)),
+            dma((frames - 1,)),
+            dma((frames - 1,)),
         ],
         compiler_params=pltpu.CompilerParams(
             vmem_limit_bytes=VMEM_BYTES, collective_id=1, has_side_effects=True
@@ -321,6 +358,18 @@
     lax.fori_loop(first, last, step, 0)
 
 
+OWN_ROWS = 9
+WINDOW = 32
+
+
+def window_start(space):
+    return jnp.minimum(lax.div(space * OWN_ROWS, 16) * 16, TILE_ROWS - WINDOW)
+
+
+def window(space):
+    return pl.ds(pl.multiple_of(window_start(space), 16), WINDOW)
+
+
 def add_into(target, terms, lead):
     count = 1
     for n in lead:
@@ -344,7 +393,7 @@
     x_ref,
     o_rows_ref,
     lse_ref,
-    g_ref,
+    g_out_ref,
     attn_space_ref,
     hidden_ref,
     attn_time_ref,
@@ -357,6 +406,9 @@
     grad_hidden_ref,
     block_out_ref,
     out_ref,
+    g_mid,
+    g_ref,
+    rows_t,
     q_aug,
     g_aug,
     q_rows,
@@ -389,6 +441,10 @@
     recv_kv,
     send_q,
     recv_q,
+    send_g,
+    recv_g,
+    send_h,
+    recv_h,
 ):
     frame, space = lax.axis_index("frame"), lax.axis_index("space")
     z, lo = lax.div(frame, 2), lax.rem(frame, 2)
@@ -414,20 +470,29 @@
     barrier = pltpu.get_barrier_semaphore()
     signal_all(barrier, peers)
 
-    for t, (rows_ref, grads_ref, offset) in enumerate(
-        [(attn_space_ref, gh_ref, c) for c in range(3)]
-        + [(hidden_ref, dqkv_ref, c) for c in range(9)]
-        + [(attn_time_ref, cot_ref, c) for c in range(3)]
+    pl.semaphore_wait(barrier, len(peers))
+    to_frames = [
+        copy(g_out_ref.at[to], g_mid.at[frame], send_g.at[n], recv_g.at[n], (to, space))
+        for n, to in enumerate(other_frames)
+    ]
+    for c in to_frames:
+        c.start()
+    g_mid[frame] = g_out_ref[frame]
+
+    for rows_ref, grads_ref, begin, tiles in (
+        (attn_space_ref, gh_ref, 0, 3),
+        (hidden_ref, dqkv_ref, 3, 9),
+        (attn_time_ref, cot_ref, 12, 3),
     ):
-        part = dot_tn(rows_ref[...], grads_ref[:, offset * TILE_COLS : (offset + 1) * TILE_COLS])
-        part = part.astype(BF)
-        for f in range(8):
-            rows = part[f * TILE_ROWS : (f + 1) * TILE_ROWS]
-            terms[f % 2, f // 2, t // 4, t // 2 % 2, t % 2] = rows
+        rows_t[...] = rows_ref[...].T
+        for n in range(tiles):
+            t = begin + n
+            part = dot(rows_t[...], grads_ref[:, n * TILE_COLS : (n + 1) * TILE_COLS]).astype(BF)
+            for f in range(8):
+                rows = part[f * TILE_ROWS : (f + 1) * TILE_ROWS]
+                terms[f % 2, f // 2, t // 4, t // 2 % 2, t % 2] = rows
     for f in range(8):
         terms[f % 2, f // 2, 3, 1, 1] = jnp.zeros((TILE_ROWS, TILE_COLS), BF)
-
-    pl.semaphore_wait(barrier, len(peers))
 
     first = [
         copy(
@@ -441,6 +506,89 @@
         for w in range(4)
     ]
     for c in first:
+        c.start()
+    for c in to_frames:
+        c.wait()
+    to_heads = [
+        copy(g_mid.at[:, to], g_ref.at[:, space], send_h.at[n], recv_h.at[n], (frame, to))
+        for n, to in enumerate(others)
+    ]
+    for c in to_heads:
+        c.start()
+    g_ref[:, space] = g_mid[:, space]
+
+    state = (q_aug, g_aug, q_rows, g_rows)
+    def attend(start, stop):
+        backward_steps(start, stop, send_step, x_ref, out_ref, *state, p_buf, ds_buf, dq_sum)
+
+    def key_grads(t):
+        to = lax.rem(space + 1 + t, 16)
+        return copy(
+            out_ref.at[to, pl.ds(1, 2)],
+            back_ref.at[space, pl.ds(1, 2)],
+            send_kv.at[t],
+            recv_kv.at[t],
+            (frame, to),
+        )
+
+    def query_grads(t):
+        to = lax.rem(space + 1 + t, 16)
+        return copy(
+            out_ref.at[to, 0], back_ref.at[space, 0], send_q.at[t], recv_q.at[t], (frame, to)
+        )
+
+    def send_step(t, stop):
+        if stop < 16:
+            key_grads(t).start()
+
+    for c in first:
+        c.wait()
+    add_into(
+        lambda y, w, a, b: half.at[y, w, a, b],
+        [lambda y, w, a, b: terms.at[y, w, a, b, core]],
+        (2, 4, 4, 2),
+    )
+    second = []
+    for i in range(1, 4):
+        to_x, to_z = lax.rem(x + i, 4), lax.rem(z + i, 4)
+        s = i - 1
+        second.append(
+            copy(half.at[0, :, to_x], x_in_a.at[s], send2.at[0, s], recv2.at[0, s], x_peer(i))
+        )
+        second.append(
+            copy(half.at[1, to_z], z_in_b.at[s], send2.at[1, s], recv2.at[1, s], z_peer(i))
+        )
+    for c in second:
+        c.start()
+    for c in to_heads:
+        c.wait()
+    backward_prepare(x_ref, o_rows_ref, lse_ref, g_ref, *state, dq_sum)
+
+    attend(0, STAGES[0])
+
+    for c in second:
+        c.wait()
+    add_into(
+        lambda w, b: half.at[0, w, x, b],
+        [lambda w, b, s=s: x_in_a.at[s, w, b] for s in range(3)],
+        (4, 2),
+    )
+    add_into(
+        lambda a, b: half.at[1, z, a, b],
+        [lambda a, b, s=s: z_in_b.at[s, a, b] for s in range(3)],
+        (4, 2),
+    )
+    third = []
+    for i in range(1, 4):
+        to_x, to_z = lax.rem(x + i, 4), lax.rem(z + i, 4)
+        s = i - 1
+        third.append(
+            copy(half.at[0, to_z, x], z_in_a.at[s], send3.at[0, s], recv3.at[0, s], z_peer(i))
+        )
+        third.append(
+            copy(half.at[1, z, to_x], x_in_b.at[s], send3.at[1, s], recv3.at[1, s], x_peer(i))
+        )
+    for c in third:
         c.start()
     moves = []
     for i, (ref, out) in enumerate(((gh_ref, grad_hidden_ref), (out_cols_ref, block_out_ref))):
@@ -457,82 +605,7 @@
             moves.append(c)
         out[frame] = rows_of(ref, frame, positions)[...]
 
-    state = (q_aug, g_aug, q_rows, g_rows)
-    backward_prepare(x_ref, o_rows_ref, lse_ref, g_ref, *state, dq_sum)
-
-    def attend(start, stop):
-        backward_steps(start, stop, send_step, x_ref, out_ref, *state, p_buf, ds_buf, dq_sum)
-
-    def key_grads(t):
-        to = lax.rem(space + 1 + t, 16)
-        return copy(
-            out_ref.at[to, pl.ds(1, 2)],
-            back_ref.at[space, pl.ds(1, 2)],
-            send_kv.at[t],
-            recv_kv.at[t],
-            (frame, to),
-        )
-
-    def query_grads(t):
-        to = lax.rem(space + 1 + t, 16)
-        return copy(
-            out_ref.at[to, 0], back_ref.at[space, 0], send_q.at[t], recv_q.at[t], (frame, to)
-        )
-
-    def send_step(t, stop):
-        if stop < 16:
-            key_grads(t).start()
-
-    attend(0, STAGES[0])
-
-    for c in first:
-        c.wait()
-    add_into(
-        lambda y, w, a, b: half.at[y, w, a, b],
-        [lambda y, w, a, b: terms.at[y, w, a, b, core]],
-        (2, 4, 4, 2),
-    )
-    second = []
-    for i in range(1, 4):
-        to_x, to_z = lax.rem(x + i, 4), lax.rem(z + i, 4)
-        s = i - 1
-        second.append(
-            copy(half.at[0, :, to_x], x_in_a.at[s], send2.at[0, s], recv2.at[0, s], x_peer(i))
-        )
-        second.append(
-            copy(half.at[1, to_z], z_in_b.at[s], send2.at[1, s], recv2.at[1, s], z_peer(i))
-        )
-    for c in second:
-        c.start()
-
     attend(STAGES[0], STAGES[1])
-
-    for c in second:
-        c.wait()
-    add_into(
-        lambda w, b: half.at[0, w, x, b],
-        [lambda w, b, s=s: x_in_a.at[s, w, b] for s in range(3)],
-        (4, 2),
-    )
-    add_into(
-        lambda a, b: half.at[1, z, a, b],
-        [lambda a, b, s=s: z_in_b.at[s, a, b] for s in range(3)],
-        (4, 2),
-    )
-    third = []
-    for i in range(1, 4):
-        to_x, to_z = lax.rem(x + i, 4), lax.rem(z + i, 4)
-        s = i - 1
-        third.append(
-            copy(half.at[0, to_z, x], z_in_a.at[s], send3.at[0, s], recv3.at[0, s], z_peer(i))
-        )
-        third.append(
-            copy(half.at[1, z, to_x], x_in_b.at[s], send3.at[1, s], recv3.at[1, s], x_peer(i))
-        )
-    for c in third:
-        c.start()
-
-    attend(STAGES[1], STAGES[2])
 
     for c in third:
         c.wait()
@@ -545,26 +618,32 @@
     fourth = copy(half.at[1 - lo, z, x], lo_in, send4.at[0], recv4.at[0], lo_peer)
     fourth.start()
 
-    attend(STAGES[2], STAGES[3])
+    attend(STAGES[1], STAGES[2])
 
     fourth.wait()
     add_into(lambda b: half.at[lo, z, x, b], [lambda b: lo_in.at[b]], (2,))
     fifth = copy(half.at[lo, z, x, 1 - hi], hi_in, send4.at[1], recv4.at[1], hi_peer)
     fifth.start()
 
-    attend(STAGES[3], 15)
+    attend(STAGES[2], 15)
     attend(15, 16)
 
     fifth.wait()
     total = (half[lo, z, x, hi].astype(F32) + hi_in[...].astype(F32)).astype(BF)
     mine[...] = total
     sixth = [
-        copy(mine, sums_ref.at[space], send6.at[i - 1], recv6.at[i - 1], space_peer(i))
+        copy(
+            mine.at[window(lax.rem(space + i, 16))],
+            sums_ref.at[space],
+            send6.at[i - 1],
+            recv6.at[i - 1],
+            space_peer(i),
+        )
         for i in range(1, 16)
     ]
     for c in sixth:
         c.start()
-    sums_ref[space] = total
+    sums_ref[space] = mine[window(space)]
 
     def finish(t, _):
         to = lax.rem(space + 1 + t, 16)
@@ -587,7 +666,7 @@
         query_grads(t).wait()
 
 
-STAGES = (3, 10, 13, 15)
+STAGES = (11, 14, 15)
 
 
 def space_backward(blocks, o_rows, lse, grads, pairs):
@@ -598,11 +677,14 @@
     dma = pltpu.SemaphoreType.DMA
     return pl.pallas_call(
         space_backward_body,
-        out_shape=(shape(blocks.shape, BF), shape((16,) + tile, BF), by_frame, by_frame),
+        out_shape=(shape(blocks.shape, BF), shape((16, WINDOW, TILE_COLS), BF), by_frame, by_frame),
         in_specs=[pl.BlockSpec(memory_space=pltpu.VMEM)] * 11,
         out_specs=[pl.BlockSpec(memory_space=pltpu.VMEM)] * 4,
         scratch_shapes=[
             pltpu.VMEM(blocks.shape, BF),
+            pltpu.VMEM(grads.shape, BF),
+            pltpu.VMEM(grads.shape, BF),
+            pltpu.VMEM((HEADS * HD, width), BF),
             pltpu.VMEM((seq, 2 * ROWS + 16), BF),
             pltpu.VMEM((seq, ROWS + 16), BF),
             pltpu.VMEM((ROWS, seq), BF),
@@ -635,6 +717,10 @@
             dma((15,)),
             dma((15,)),
             dma((15,)),
+            dma((7,)),
+            dma((7,)),
+            dma((15,)),
+            dma((15,)),
         ],
         compiler_params=pltpu.CompilerParams(
             vmem_limit_bytes=VMEM_BYTES, collective_id=0, has_side_effects=True
@@ -723,35 +809,24 @@
     )
 
 
-def exchange(blocks, axis):
-    return lax.all_to_all(blocks, axis, split_axis=0, concat_axis=0, tiled=True)
-
-
-def exchange_all(blocks):
-    flat = exchange(blocks.reshape((-1,) + blocks.shape[2:]), ALL)
-    return flat.reshape(blocks.shape)
-
-
 def shards(
     hidden_in, query_space, key_space, value_space, cotangent, w_space_out, w_time_qkv, w_time_out
 ):
     width = hidden_in.shape[2]
     frames = lax.axis_size("frame")
-    head_blocks, hidden_cols, cot_cols, mixed, o_rows, lse = space_forward(
+    head_blocks, hidden_cols, cot_cols, attn, o_rows, lse = space_forward(
         query_space, key_space, value_space, hidden_in, cotangent, frames
     )
-    attn = exchange_all(mixed)
     g_out, grad_cols, out_cols, attn_space, hidden, attn_time, dqkv = middle(
         attn, hidden_cols, cot_cols, w_space_out, w_time_qkv, w_time_out
     )
-    grads = exchange_all(g_out)
     pairs = (attn_space, hidden, attn_time, grad_cols, dqkv, cot_cols.reshape(-1, width), out_cols)
-    back, sums, grad_hidden, block_out = space_backward(head_blocks, o_rows, lse, grads, pairs)
+    back, sums, grad_hidden, block_out = space_backward(head_blocks, o_rows, lse, g_out, pairs)
     block_out = block_out.reshape(hidden_in.shape)
     grad_hidden = grad_hidden.reshape(hidden_in.shape)
-    rows_dev = TILE_ROWS // HEADS
-    own = lax.dynamic_slice_in_dim(sums, lax.axis_index("space") * rows_dev, rows_dev, 1)
-    own = own.transpose(1, 0, 2).reshape(rows_dev, -1).astype(F32)
+    space = lax.axis_index("space")
+    own = lax.dynamic_slice_in_dim(sums, space * OWN_ROWS - window_start(space), OWN_ROWS, 1)
+    own = own.transpose(1, 0, 2).reshape(OWN_ROWS, -1).astype(F32)
     cuts = (own[:, :width], own[:, width : 4 * width], own[:, 4 * width : 5 * width])
     return (block_out, grad_hidden, *join_heads(back), *cuts)
 

time: 293 us -> 244 us (0.83)
  blocking collectives: 27.2 us -> 0 us
  waiting for transfers between devices: 19.1 us -> 0 us
  Pallas kernels: 232 us -> 237 us
  starting transfers between devices: 4.61 us -> 0 us
    all_to_all x1 -> x0, blocking collectives: 27.2 us -> none  [exchange(): return lax.all_to_all(blocks, axis, split_axis=0, concat_axis=0, tiled=True)]
    all_to_all x1 -> x0, waiting for transfers between devices: 19.1 us -> none  [exchange(): return lax.all_to_all(blocks, axis, split_axis=0, concat_axis=0, tiled=True)]
    pallas_call x1, Pallas kernels: 58.3 us -> 74.7 us  [space_forward(): pl.pallas_call(space_forward_body, out_shape=(shape((HEADS, 3, ROWS, toke...]
    pallas_call x2, Pallas kernels: 41.4 us -> 30.3 us  [kernel_call(): pl.pallas_call(body, out_shape=out_shape, scratch_shapes=scratch_shapes,...]
    all_to_all x1 -> x0, starting transfers between devices: 4.61 us -> none  [exchange(): return lax.all_to_all(blocks, axis, split_axis=0, concat_axis=0, tiled=True)]
  transfers between devices with their start and end apart: 1 -> 0, of which waited for: 1 -> 0; matrix products, arithmetic and copies ran while one was open for 0% -> 0% of each run, Pallas kernels for 0% -> 0%
where the time goes in v4:
time: 244 us; the launch traced here: 241 us
  Pallas kernels  237 us (97%)
  local copies, waits for them, and re-layouts  3.23 us (1%)
    pallas_call x1, Pallas kernels, space_backward(): pl.pallas_call(space_backward_body, out_shape=(shape(blocks.shape, BF), s...  131 us
    pallas_call x1, Pallas kernels, space_forward(): pl.pallas_call(space_forward_body, out_shape=(shape((HEADS, 3, ROWS, toke...  74.7 us
    pallas_call x2, Pallas kernels, kernel_call(): pl.pallas_call(body, out_shape=out_shape, scratch_shapes=scratch_shapes,...  30.3 us

profile of v4, /device:TPU:1, one launch (start us, length us, event | category | flops | bytes accessed | tf_op | source)
XLA Modules:
  0.0 240.7 jit_solution(9385786611213385278)
XLA Ops:
  0.6 74.7 %shard_map.143 = (bf16[16,3,80,256]{3,2,1,0:T(8,128)(2,1)}, bf16[8,32,1152]{2,1,0:T(8,128)(2,1)}, bf16[8,32,1152]{2,1,0:T(8,128)(2,1)}, bf16[8,16,32,128]{3,2,1,...) custom-call(bf16[1,256,1152]{2,1,0:T(8,128)(2,1)} %q_ref.1, bf16[1,256,1152]{2,1,0:T(8,128)(2,1)} %k_ref.1, ...), custom_call_target="tpu_custom_call" | custom-call | flops 8589934592 | bytes 8388608 | tf_op jit(solution)/shard_map/pallas_call | solution.py:268
  75.3 27.3 %shard_map.144 = (bf16[8,16,32,128]{3,2,1,0:T(8,128)(2,1)}, bf16[256,1152]{1,0:T(8,128)(2,1)}, bf16[256,1152]{1,0:T(8,128)(2,1)}, bf16[256,1152]{1,0:T(8,128)(2,...) custom-call(bf16[8,16,32,128]{3,2,1,0:T(8,128)(2,1)} %get-tuple-element.31.attn_ref, ...), custom_call_target="tpu_custom_call" | custom-call | flops 6794772480 | bytes 20971520 | tf_op jit(solution)/shard_map/pallas_call | solution.py:20
  102.7 131.5 %shard_map.145 = (bf16[16,3,80,256]{3,2,1,0:T(8,128)(2,1)}, bf16[16,32,384]{2,1,0:T(8,128)(2,1)}, bf16[8,32,1152]{2,1,0:T(8,128)(2,1)}, bf16[8,32,1152]{2,1,0:T(8,128)(2,1)}) custom-call(bf16[16,3,80,256]{3,2,1,0:T(8,128)(2,1)} %get-tuple-element.28.x_ref, f32[16,80,256]{2,1,0:T(8,128)} %get-tuple-element.29.o_rows_ref, ...), custom_call_target="tpu_custom_call" | custom-call | flops 21474836480 | bytes 16777216 | tf_op jit(solution)/shard_map/pallas_call | solution.py:678
  234.1 0.0 copy-start.2
  234.1 3.0 %shard_map.146 = (bf16[1,256,1152]{2,1,0:T(8,128)(2,1)}, bf16[1,256,1152]{2,1,0:T(8,128)(2,1)}, bf16[1,256,1152]{2,1,0:T(8,128)(2,1)}) custom-call(bf16[16,3,80,256]{3,2,1,0:T(8,128)(2,1)} %get-tuple-element.43.in_ref), custom_call_target="tpu_custom_call" | custom-call | bytes 4423680 | tf_op jit(solution)/shard_map/pallas_call | solution.py:20
  237.2 0.0 copy-start.1
  237.2 0.0 copy-done.2
  237.2 0.1 convert_bitcast_fusion
  237.2 0.0 copy-start
  237.2 0.1 copy.16
  237.4 0.1 copy.17
  237.5 0.7 slice.13
  238.2 0.7 fusion
  238.9 0.0 copy-done.1
  238.9 0.8 copy.20
  239.7 0.0 copy-done
  239.7 0.8 copy.21
  (1 shorter events, 0.0 us)
Async XLA Ops:
  234.1 3.1 %copy-start.2 = (bf16[16,32,384]{2,1,0:T(8,128)(2,1)S(1)}, bf16[16,32,384]{2,1,0:T(8,128)(2,1)}, u32[]{:S(2)}) copy-start(bf16[16,32,384]{2,1,0:T(8,128)(2,1)} %get-tuple-element.47) | copy-start | bytes 1179652
  237.2 1.7 copy-start.1
  237.2 2.4 %copy-start = (bf16[8,32,1152]{2,1,0:T(8,128)(2,1)S(1)}, bf16[8,32,1152]{2,1,0:T(8,128)(2,1)}, u32[]{:S(2)}) copy-start(bf16[8,32,1152]{2,1,0:T(8,128)(2,1)} %get-tuple-element.42) | copy-start | bytes 1769476

commit v5 on v4

--- a/solution.py
+++ b/solution.py
@@ -305,6 +305,7 @@
 
 Q_STEP = 1024
 TILE_ROWS = 144
+PART_ROWS = 48
 TILE_COLS = 384
 
 
@@ -418,21 +419,18 @@
     dq_sum,
     terms,
     half,
-    x_in_a,
-    z_in_b,
-    z_in_a,
-    x_in_b,
-    lo_in,
-    hi_in,
+    in_a1,
+    in_b1,
+    in_c1,
+    in_a2,
+    in_b2,
+    in_c2,
+    in_3,
     mine,
     send1,
     recv1,
-    send2,
-    recv2,
-    send3,
-    recv3,
-    send4,
-    recv4,
+    sends,
+    recvs,
     send6,
     recv6,
     send_f,
@@ -459,14 +457,19 @@
     def space_peer(i):
         return (frame, lax.rem(space + i, 16))
 
-    lo_peer = (z * 2 + 1 - lo, space)
-    hi_peer = (frame, x * 4 + (1 - hi) * 2 + core)
+    def y_index(i):
+        return (1 - lo if i % 2 else lo), (1 - hi if i // 2 else hi)
+
+    def y_peer(i):
+        to_lo, to_hi = y_index(i)
+        return (z * 2 + to_lo, x * 4 + to_hi * 2 + core)
+
     core_peer = (frame, x * 4 + hi * 2 + 1 - core)
-
     copy = copy_to
     others = [lax.rem(space + i, 16) for i in range(1, 16)]
     other_frames = [lax.rem(frame + i, 8) for i in range(1, 8)]
     peers = [(frame, to) for to in others] + [(to, space) for to in other_frames]
+    peers.append(y_peer(3))
     barrier = pltpu.get_barrier_semaphore()
     signal_all(barrier, peers)
 
@@ -479,6 +482,25 @@
         c.start()
     g_mid[frame] = g_out_ref[frame]
 
+    first = []
+
+    def store_terms(t, part):
+        for f in range(8):
+            for p in range(3):
+                begin = f * TILE_ROWS + p * PART_ROWS
+                terms[p, t // 4, f % 2, f // 2, t // 2 % 2, t % 2] = part[begin : begin + PART_ROWS]
+        if t % 4 == 3:
+            for p in range(3):
+                c = copy(
+                    terms.at[p, t // 4, :, :, :, 1 - core],
+                    half.at[p, t // 4],
+                    send1.at[p, t // 4],
+                    recv1.at[p, t // 4],
+                    core_peer,
+                )
+                c.start()
+                first.append(c)
+
     for rows_ref, grads_ref, begin, tiles in (
         (attn_space_ref, gh_ref, 0, 3),
         (hidden_ref, dqkv_ref, 3, 9),
@@ -486,27 +508,10 @@
     ):
         rows_t[...] = rows_ref[...].T
         for n in range(tiles):
-            t = begin + n
-            part = dot(rows_t[...], grads_ref[:, n * TILE_COLS : (n + 1) * TILE_COLS]).astype(BF)
-            for f in range(8):
-                rows = part[f * TILE_ROWS : (f + 1) * TILE_ROWS]
-                terms[f % 2, f // 2, t // 4, t // 2 % 2, t % 2] = rows
-    for f in range(8):
-        terms[f % 2, f // 2, 3, 1, 1] = jnp.zeros((TILE_ROWS, TILE_COLS), BF)
-
-    first = [
-        copy(
-            terms.at[y, w, :, :, 1 - core],
-            half.at[y, w],
-            send1.at[y, w],
-            recv1.at[y, w],
-            core_peer,
-        )
-        for y in range(2)
-        for w in range(4)
-    ]
-    for c in first:
-        c.start()
+            part = dot(rows_t[...], grads_ref[:, n * TILE_COLS : (n + 1) * TILE_COLS])
+            store_terms(begin + n, part.astype(BF))
+    store_terms(15, jnp.zeros((8 * TILE_ROWS, TILE_COLS), BF))
+
     for c in to_frames:
         c.wait()
     to_heads = [
@@ -544,52 +549,62 @@
     for c in first:
         c.wait()
     add_into(
-        lambda y, w, a, b: half.at[y, w, a, b],
-        [lambda y, w, a, b: terms.at[y, w, a, b, core]],
-        (2, 4, 4, 2),
-    )
-    second = []
-    for i in range(1, 4):
-        to_x, to_z = lax.rem(x + i, 4), lax.rem(z + i, 4)
-        s = i - 1
-        second.append(
-            copy(half.at[0, :, to_x], x_in_a.at[s], send2.at[0, s], recv2.at[0, s], x_peer(i))
-        )
-        second.append(
-            copy(half.at[1, to_z], z_in_b.at[s], send2.at[1, s], recv2.at[1, s], z_peer(i))
-        )
-    for c in second:
-        c.start()
+        lambda p, a, y, w: half.at[p, a, y, w],
+        [lambda p, a, y, w: terms.at[p, a, y, w, :, core]],
+        (3, 4, 2, 4),
+    )
+
+    def stage(n, along_x, along_z, along_y):
+        started = []
+        for i in range(1, 4):
+            for source, slots, index, peer in (
+                (*along_x, lax.rem(x + i, 4), x_peer(i)),
+                (*along_z, lax.rem(z + i, 4), z_peer(i)),
+                (*along_y, y_index(i), y_peer(i)),
+            ):
+                at = len(started)
+                started.append(
+                    copy(source(index), slots(i - 1), sends.at[n, at], recvs.at[n, at], peer)
+                )
+        for c in started:
+            c.start()
+        return started
+
+    def add_all(started, *sums):
+        for c in started:
+            c.wait()
+        for target, slots, lead in sums:
+            add_into(target, [lambda *at, k=k: slots(k, *at) for k in range(3)], lead)
+
+    a1 = lambda k, *at: in_a1.at[(k, *at)]
+    b1 = lambda k, *at: in_b1.at[(k, *at)]
+    c1 = lambda k, *at: in_c1.at[(k, *at)]
+    a2 = lambda k, *at: in_a2.at[(k, *at)]
+    b2 = lambda k, *at: in_b2.at[(k, *at)]
+    c2 = lambda k, *at: in_c2.at[(k, *at)]
+
+    started = stage(
+        0,
+        (lambda i: half.at[0, i], a1),
+        (lambda i: half.at[1, :, :, i], b1),
+        (lambda i: half.at[2, :, i[0], :, i[1]], c1),
+    )
     for c in to_heads:
         c.wait()
     backward_prepare(x_ref, o_rows_ref, lse_ref, g_ref, *state, dq_sum)
-
     attend(0, STAGES[0])
-
-    for c in second:
-        c.wait()
-    add_into(
-        lambda w, b: half.at[0, w, x, b],
-        [lambda w, b, s=s: x_in_a.at[s, w, b] for s in range(3)],
-        (4, 2),
-    )
-    add_into(
-        lambda a, b: half.at[1, z, a, b],
-        [lambda a, b, s=s: z_in_b.at[s, a, b] for s in range(3)],
-        (4, 2),
-    )
-    third = []
-    for i in range(1, 4):
-        to_x, to_z = lax.rem(x + i, 4), lax.rem(z + i, 4)
-        s = i - 1
-        third.append(
-            copy(half.at[0, to_z, x], z_in_a.at[s], send3.at[0, s], recv3.at[0, s], z_peer(i))
-        )
-        third.append(
-            copy(half.at[1, z, to_x], x_in_b.at[s], send3.at[1, s], recv3.at[1, s], x_peer(i))
-        )
-    for c in third:
-        c.start()
+    add_all(
+        started,
+        (lambda y, w: half.at[0, x, y, w], a1, (2, 4)),
+        (lambda a, y: half.at[1, a, y, z], b1, (4, 2)),
+        (lambda a, w: half.at[2, a, lo, w, hi], c1, (4, 4)),
+    )
+    started = stage(
+        1,
+        (lambda i: half.at[2, i, lo, :, hi], c2),
+        (lambda i: half.at[0, x, :, i], a2),
+        (lambda i: half.at[1, :, i[0], z, i[1]], b2),
+    )
     moves = []
     for i, (ref, out) in enumerate(((gh_ref, grad_hidden_ref), (out_cols_ref, block_out_ref))):
         positions = out.shape[1]
@@ -606,31 +621,26 @@
         out[frame] = rows_of(ref, frame, positions)[...]
 
     attend(STAGES[0], STAGES[1])
-
-    for c in third:
+    add_all(
+        started,
+        (lambda y: half.at[0, x, y, z], a2, (2,)),
+        (lambda a: half.at[1, a, lo, z, hi], b2, (4,)),
+        (lambda w: half.at[2, x, lo, w, hi], c2, (4,)),
+    )
+    started = stage(
+        2,
+        (lambda i: half.at[1, i, lo, z, hi], lambda k: in_3.at[1, k]),
+        (lambda i: half.at[2, x, lo, i, hi], lambda k: in_3.at[2, k]),
+        (lambda i: half.at[0, x, i[0], z, i[1]], lambda k: in_3.at[0, k]),
+    )
+    attend(STAGES[1], STAGES[2])
+    for c in started:
         c.wait()
-    add_into(
-        lambda b: half.at[0, z, x, b], [lambda b, s=s: z_in_a.at[s, b] for s in range(3)], (2,)
-    )
-    add_into(
-        lambda b: half.at[1, z, x, b], [lambda b, s=s: x_in_b.at[s, b] for s in range(3)], (2,)
-    )
-    fourth = copy(half.at[1 - lo, z, x], lo_in, send4.at[0], recv4.at[0], lo_peer)
-    fourth.start()
-
-    attend(STAGES[1], STAGES[2])
-
-    fourth.wait()
-    add_into(lambda b: half.at[lo, z, x, b], [lambda b: lo_in.at[b]], (2,))
-    fifth = copy(half.at[lo, z, x, 1 - hi], hi_in, send4.at[1], recv4.at[1], hi_peer)
-    fifth.start()
-
-    attend(STAGES[2], 15)
-    attend(15, 16)
-
-    fifth.wait()
-    total = (half[lo, z, x, hi].astype(F32) + hi_in[...].astype(F32)).astype(BF)
-    mine[...] = total
+    for p in range(3):
+        total = half[p, x, lo, z, hi].astype(F32)
+        for k in range(3):
+            total = total + in_3[p, k].astype(F32)
+        mine[p * PART_ROWS : (p + 1) * PART_ROWS] = total.astype(BF)
     sixth = [
         copy(
             mine.at[window(lax.rem(space + i, 16))],
@@ -644,6 +654,8 @@
     for c in sixth:
         c.start()
     sums_ref[space] = mine[window(space)]
+    attend(STAGES[2], 15)
+    attend(15, 16)
 
     def finish(t, _):
         to = lax.rem(space + 1 + t, 16)
@@ -666,13 +678,13 @@
         query_grads(t).wait()
 
 
-STAGES = (11, 14, 15)
+STAGES = (9, 12, 14)
 
 
 def space_backward(blocks, o_rows, lse, grads, pairs):
     count, _, _, width = blocks.shape
     seq = count * width
-    tile = (TILE_ROWS, TILE_COLS)
+    part = (PART_ROWS, TILE_COLS)
     by_frame = shape((8, width // 8, HEADS * HD), BF)
     dma = pltpu.SemaphoreType.DMA
     return pl.pallas_call(
@@ -692,23 +704,20 @@
             pltpu.VMEM((seq, width), BF),
             pltpu.VMEM((seq, width), BF),
             pltpu.VMEM((seq, ROWS), F32),
-            pltpu.VMEM((2, 4, 4, 2, 2) + tile, BF),
-            pltpu.VMEM((2, 4, 4, 2) + tile, BF),
-            pltpu.VMEM((3, 4, 2) + tile, BF),
-            pltpu.VMEM((3, 4, 2) + tile, BF),
-            pltpu.VMEM((3, 2) + tile, BF),
-            pltpu.VMEM((3, 2) + tile, BF),
-            pltpu.VMEM((2,) + tile, BF),
-            pltpu.VMEM(tile, BF),
-            pltpu.VMEM(tile, BF),
-            dma((2, 4)),
-            dma((2, 4)),
-            dma((2, 3)),
-            dma((2, 3)),
-            dma((2, 3)),
-            dma((2, 3)),
-            dma((2,)),
-            dma((2,)),
+            pltpu.VMEM((3, 4, 2, 4, 2, 2) + part, BF),
+            pltpu.VMEM((3, 4, 2, 4, 2) + part, BF),
+            pltpu.VMEM((3, 2, 4, 2) + part, BF),
+            pltpu.VMEM((3, 4, 2, 2) + part, BF),
+            pltpu.VMEM((3, 4, 4) + part, BF),
+            pltpu.VMEM((3, 2, 2) + part, BF),
+            pltpu.VMEM((3, 4) + part, BF),
+            pltpu.VMEM((3, 4) + part, BF),
+            pltpu.VMEM((3, 3) + part, BF),
+            pltpu.VMEM((TILE_ROWS, TILE_COLS), BF),
+            dma((3, 4)),
+            dma((3, 4)),
+            dma((3, 9)),
+            dma((3, 9)),
             dma((15,)),
             dma((15,)),
             dma((2, 7)),

time: 244 us -> 228 us (0.934)
  Pallas kernels: 237 us -> 220 us
    pallas_call x1, Pallas kernels: 131 us -> 115 us  [space_backward(): pl.pallas_call(space_backward_body, out_shape=(shape(blocks.shape, BF), s...]
where the time goes in v5:
time: 228 us; the launch traced here: 224 us
  Pallas kernels  220 us (96%)
  local copies, waits for them, and re-layouts  3.23 us (1%)
    pallas_call x1, Pallas kernels, space_backward(): pl.pallas_call(space_backward_body, out_shape=(shape(blocks.shape, BF), s...  115 us
    pallas_call x1, Pallas kernels, space_forward(): pl.pallas_call(space_forward_body, out_shape=(shape((HEADS, 3, ROWS, toke...  74.7 us
    pallas_call x2, Pallas kernels, kernel_call(): pl.pallas_call(body, out_shape=out_shape, scratch_shapes=scratch_shapes,...  30.3 us

profile of v5, /device:TPU:1, one launch (start us, length us, event | category | flops | bytes accessed | tf_op | source)
XLA Modules:
  0.0 224.3 jit_solution(17268177988976349061)
XLA Ops:
  0.6 74.7 %shard_map.143 = (bf16[16,3,80,256]{3,2,1,0:T(8,128)(2,1)}, bf16[8,32,1152]{2,1,0:T(8,128)(2,1)}, bf16[8,32,1152]{2,1,0:T(8,128)(2,1)}, bf16[8,16,32,128]{3,2,1,...) custom-call(bf16[1,256,1152]{2,1,0:T(8,128)(2,1)} %q_ref.1, bf16[1,256,1152]{2,1,0:T(8,128)(2,1)} %k_ref.1, ...), custom_call_target="tpu_custom_call" | custom-call | flops 8589934592 | bytes 8388608 | tf_op jit(solution)/shard_map/pallas_call | solution.py:268
  75.3 27.3 %shard_map.144 = (bf16[8,16,32,128]{3,2,1,0:T(8,128)(2,1)}, bf16[256,1152]{1,0:T(8,128)(2,1)}, bf16[256,1152]{1,0:T(8,128)(2,1)}, bf16[256,1152]{1,0:T(8,128)(2,...) custom-call(bf16[8,16,32,128]{3,2,1,0:T(8,128)(2,1)} %get-tuple-element.31.attn_ref, ...), custom_call_target="tpu_custom_call" | custom-call | flops 6794772480 | bytes 20971520 | tf_op jit(solution)/shard_map/pallas_call | solution.py:20
  102.7 115.0 %shard_map.145 = (bf16[16,3,80,256]{3,2,1,0:T(8,128)(2,1)}, bf16[16,32,384]{2,1,0:T(8,128)(2,1)}, bf16[8,32,1152]{2,1,0:T(8,128)(2,1)}, bf16[8,32,1152]{2,1,0:T(8,128)(2,1)}) custom-call(bf16[16,3,80,256]{3,2,1,0:T(8,128)(2,1)} %get-tuple-element.28.x_ref, f32[16,80,256]{2,1,0:T(8,128)} %get-tuple-element.29.o_rows_ref, ...), custom_call_target="tpu_custom_call" | custom-call | flops 21474836480 | bytes 16777216 | tf_op jit(solution)/shard_map/pallas_call | solution.py:690
  217.7 0.0 copy-start.2
  217.7 3.0 %shard_map.146 = (bf16[1,256,1152]{2,1,0:T(8,128)(2,1)}, bf16[1,256,1152]{2,1,0:T(8,128)(2,1)}, bf16[1,256,1152]{2,1,0:T(8,128)(2,1)}) custom-call(bf16[16,3,80,256]{3,2,1,0:T(8,128)(2,1)} %get-tuple-element.43.in_ref), custom_call_target="tpu_custom_call" | custom-call | bytes 4423680 | tf_op jit(solution)/shard_map/pallas_call | solution.py:20
  220.7 0.0 copy-start.1
  220.7 0.0 copy-done.2
  220.7 0.1 convert_bitcast_fusion
  220.8 0.0 copy-start
  220.8 0.1 copy.16
  220.9 0.1 copy.17
  221.0 0.7 slice.13
  221.7 0.7 fusion
  222.4 0.0 copy-done.1
  222.4 0.8 copy.20
  223.2 0.0 copy-done
  223.2 0.8 copy.21
  (1 shorter events, 0.0 us)
Async XLA Ops:
  217.7 3.1 %copy-start.2 = (bf16[16,32,384]{2,1,0:T(8,128)(2,1)S(1)}, bf16[16,32,384]{2,1,0:T(8,128)(2,1)}, u32[]{:S(2)}) copy-start(bf16[16,32,384]{2,1,0:T(8,128)(2,1)} %get-tuple-element.47) | copy-start | bytes 1179652
  220.7 1.7 copy-start.1
  220.8 2.4 %copy-start = (bf16[8,32,1152]{2,1,0:T(8,128)(2,1)S(1)}, bf16[8,32,1152]{2,1,0:T(8,128)(2,1)}, u32[]{:S(2)}) copy-start(bf16[8,32,1152]{2,1,0:T(8,128)(2,1)} %get-tuple-element.42) | copy-start | bytes 1769476
